TPU v7x, 512 devices: a whole 4x4x16 slice. The times are simulated.
512 devices in a mesh: ma: 32 (over z, core), row: 16 (over y, x).
Axes of the slice: x: 4, y: 4, z: 16, core: 2. Of those that a mesh axis runs over, the one named last changes fastest.
Arguments:
- seed_field: bfloat16 [4, 16, 2, 1024, 1024], P(None, 'row', None, 'ma'), may hold values from -6 to 6
- cotangent: bfloat16 [2, 16, 2, 1024, 1024], P(None, 'row', None, 'ma'), may hold values from -6 to 6
- step_size: float32 [1], replicated, may hold values from 0.25 to 1
- owner_list: int32 [1024], replicated, may hold values from 0 to 1023, as said below
Outputs:
- nonlinear: float32 [2, 16, 2, 1024, 1024], P(None, 'row', None, 'ma')
- seed_next: float32 [4, 16, 2, 1024, 1024], P(None, 'row', None, 'ma')
Inputs may be any that keep to these rules, and one draw needn't show every extreme that they name: owner_list is a permutation of the wavenumbers; entries 32 d to 32 (d + 1) - 1 name the wavenumbers of owner d, and a block that holds m also holds 1023 - m.
All inputs are finite; a program needn't handle non-finite values.
Results may differ from a plain program's by a relative error of at most 0.0082.
Values may be sent and summed in bfloat16 or wider, within the bound.
A program may use at most 64 MiB of HBM per device.

v0:
```python
import math

import jax
import jax.numpy as jnp
from jax import lax
from jax.sharding import PartitionSpec as P

WAVES = 1024
DEGREES = 1024
NLAT = 1024
NLON = 2048


def with_halo(cells, sides, width):
    for axis, dim in sides:
        count = lax.axis_size(axis)
        ends = count - 1
        head = lax.slice_in_dim(cells, 0, width, axis=dim)
        tail = lax.slice_in_dim(cells, cells.shape[dim] - width, cells.shape[dim], axis=dim)
        cells = jnp.concatenate(
            [
                lax.ppermute(tail, axis, [(i, (i + 1) % count) for i in range(ends)]),
                cells,
                lax.ppermute(head, axis, [((i + 1) % count, i) for i in range(ends)]),
            ],
            axis=dim,
        )
    return cells


def lat_cosines(theta_index):
    degree = jnp.arange(DEGREES, dtype=jnp.int32)
    phase_index = (2 * theta_index[:, None] + 1) * degree[None, :] % (4 * NLAT)
    return jnp.cos(phase_index.astype(jnp.float32) * (math.pi / (2 * NLAT))).astype(jnp.bfloat16)


def wave_cosines(wave_ids):
    points = jnp.arange(NLON, dtype=jnp.int32)
    phase_index = wave_ids[:, None] * points[None, :] % NLON
    angles = phase_index.astype(jnp.float32) * (2.0 * math.pi / NLON)
    return jnp.stack([jnp.cos(angles), -jnp.sin(angles)]).astype(jnp.bfloat16)


def local(seed_field, cotangent, step_size, owner_list):
    own_waves = cotangent.shape[3]
    norm_scale = 2.0 / math.sqrt(DEGREES * WAVES)
    block_width = min(128, WAVES)
    my_waves = lax.dynamic_slice_in_dim(owner_list, lax.axis_index("ma") * own_waves, own_waves)
    degree = jnp.arange(DEGREES, dtype=jnp.int32)
    live_cols = degree[:, None] >= my_waves[None, :]
    live_rows = jnp.transpose(live_cols)
    zero_value = jnp.zeros((), jnp.bfloat16)
    listed = jnp.take(seed_field, owner_list, axis=4)
    owned_seed = lax.all_to_all(listed, "ma", split_axis=4, concat_axis=3, tiled=True)
    lat_table = lat_cosines(jnp.arange(NLAT, dtype=jnp.int32))
    forward_rows = jnp.einsum(
        "crslk,tl->crstk",
        jnp.where(live_cols, owned_seed, zero_value),
        lat_table,
        preferred_element_type=jnp.float32,
    )
    adjoint_rows = jnp.einsum(
        "crskl,tl->crstk",
        jnp.where(live_rows, cotangent, zero_value),
        lat_table,
        preferred_element_type=jnp.float32,
    )
    spec_rows = jnp.concatenate([forward_rows, adjoint_rows], axis=0).astype(jnp.bfloat16)
    gridded = lax.all_to_all(spec_rows, "ma", split_axis=3, concat_axis=4, tiled=True)
    grid_field = None
    for start in range(0, WAVES, block_width):
        wave_block = wave_cosines(owner_list[start : start + block_width])
        partial_grid = jnp.einsum(
            "crsjm,smf->crjf",
            gridded[..., start : start + block_width],
            wave_block,
            preferred_element_type=jnp.float32,
        )
        grid_field = partial_grid if grid_field is None else grid_field + partial_grid
    grid_field = norm_scale * grid_field
    radial_pair = jnp.stack([grid_field[1], grid_field[3]])
    padded = with_halo(radial_pair, (("row", 1),), 1)
    slopes = 0.5 * (padded[:, 2:] - padded[:, :-2])
    vel_tor = grid_field[0]
    mag_tor = grid_field[2]
    adj_vel = grid_field[4]
    adj_mag = grid_field[5]
    vel_pol = slopes[0]
    mag_pol = slopes[1]
    term_vel = mag_tor * mag_pol - vel_tor * vel_pol
    term_mag = vel_tor * mag_pol - vel_pol * mag_tor
    grad_vtor = -vel_pol * adj_vel + mag_pol * adj_mag
    grad_vpol = -vel_tor * adj_vel - mag_tor * adj_mag
    grad_mtor = mag_pol * adj_vel - vel_pol * adj_mag
    grad_mpol = mag_tor * adj_vel + vel_tor * adj_mag
    cotangent_pair = jnp.stack([grad_vpol, grad_mpol])
    padded_back = with_halo(cotangent_pair, (("row", 1),), 1)
    back_slopes = 0.5 * (padded_back[:, :-2] - padded_back[:, 2:])
    analysis_in = jnp.stack(
        [term_vel, term_mag, grad_vtor, back_slopes[0], grad_mtor, back_slopes[1]]
    ).astype(jnp.bfloat16)
    spectra_parts = []
    for start in range(0, WAVES, block_width):
        wave_block = wave_cosines(owner_list[start : start + block_width])
        spectra_parts.append(
            jnp.einsum(
                "crjf,smf->crsjm", analysis_in, wave_block, preferred_element_type=jnp.float32
            )
        )
    spectra = (norm_scale * jnp.concatenate(spectra_parts, axis=4)).astype(jnp.bfloat16)
    position = jnp.arange(NLAT, dtype=jnp.int32)
    returned = lax.all_to_all(spectra, "ma", split_axis=4, concat_axis=3, tiled=True)
    back_table = lat_cosines(position)
    result = jnp.einsum("crstk,tl->crskl", returned, back_table, preferred_element_type=jnp.float32)
    result = jnp.where(live_rows, result, 0.0)
    nonlinear = result[:2]
    seed_next = jnp.swapaxes(owned_seed, 3, 4).astype(jnp.float32) - step_size[0] * result[2:]
    return (nonlinear, seed_next)


def solution(mesh):
    return jax.shard_map(
        local,
        mesh=mesh,
        in_specs=(P(None, "row", None, "ma", None), P(None, "row", None, "ma", None), P(), P()),
        out_specs=(P(None, "row", None, "ma", None), P(None, "row", None, "ma", None)),
        check_vma=False,
    )
```

profile of v0, /device:TPU:1, one launch (start us, length us, event | category | flops | bytes accessed | tf_op | source)
XLA Modules:
  0.0 313.1 jit_solution(7844892380250730172)
XLA Ops:
  4.9 8.9 %gather_fusion = bf16[1024,4,2,32]{3,1,2,0:T(4,128)(2,1)} fusion(bf16[4,2,32,1024]{2,0,3,1:T(4,128)(2,1)S(1)} %bitcast.362, s32[1024]{0:T(1024)S(1)} %fusion.140), kind=kCustom, calls=%fused_computation | custom fusion | bytes 1052672 | tf_op jit(solution)/shard_map/jit(_take)/gather | solution.py:53
  13.7 5.2 %fusion.173 = bf16[1024,1,2,4,32]{4,3,2,1,0:T(4,128)(2,1)S(1)} fusion(bf16[1024,4,2,32]{3,1,2,0:T(4,128)(2,1)} %gather_fusion, pred[1024]{0:T(1024)(128)(4,1)S(1)} %compare_and_fusion), kind=kLoop, calls=%fused_computation.271 | loop fusion | flops 262144 | bytes 1049600
  21.7 17.4 %all-to-all-start = ((bf16[32,2,4096]{2,1,0:T(2,128)(2,1)}), bf16[32,2,4096]{2,1,0:T(2,128)(2,1)S(1)}, u32[]{:S(2)}, u32[]{:S(2)}) async-start(bf16[32,2,4096]{2,1,0:T(2,128)(2,1)} %reshape.1275), calls=%async_computation | async-start | bytes 1048576 | tf_op jit(solution)/shard_map/all_to_all | solution.py:54
  39.4 16.2 %fusion.45 = bf16[2,1,2,1024,32]{3,4,2,0,1:T(8,128)(2,1)S(1)} fusion(s32[1024]{0:T(1024)S(1)} %multiply_add_fusion.1, bf16[2,1,2,32,1024]{4,3,2,1,0:T(8,128)(2,1)S(1)} %copy-done.18, pred[32,1024]{1,0:T(8,128)(4,1)S(1)} %iota_compare_fusion.1), kind=kOutput, calls=%fused_computation.75 | convolution fusion | flops 284426240 | bytes 561152 | tf_op jit(solution)/shard_map/crskl,tl->crstk/dot_general | solution.py:62
  55.5 16.9 %all-to-all-done = bf16[32,2,4096]{2,1,0:T(2,128)(2,1)S(1)} async-done(((bf16[32,2,4096]{2,1,0:T(2,128)(2,1)}), bf16[32,2,4096]{2,1,0:T(2,128)(2,1)S(1)}, u32[]{:S(2)}, u32[]{:S(2)}) %all-to-all-start) | async-done | bytes 524320 | tf_op jit(solution)/shard_map/all_to_all | solution.py:54
  73.5 4.0 %fusion.171 = (f32[4,1,2,32,32,32]{4,3,5,2,0,1:T(8,128)}, bf16[4,1,2,32,32,32]{4,3,5,2,0,1:T(8,128)(2,1)}) fusion(bf16[4,1,2,32,32,32]{3,0,2,5,4,1:T(4,128)(2,1)S(1)} %bitcast.361), kind=kLoop, calls=%fused_computation.269 | loop fusion | flops 262144 | bytes 2097152 | tf_op jit(solution)/shard_map/convert_element_type | solution.py:117
  77.5 3.5 %all_to_all.40 = bf16[4,2,1024,32]{2,3,1,0:T(8,128)(2,1)S(1)} reshape(bf16[4,1,2,32,32,32]{4,3,5,2,0,1:T(8,128)(2,1)} %get-tuple-element.11) | data formatting | bytes 1048576 | tf_op jit(solution)/shard_map/all_to_all | solution.py:54
  81.0 16.3 %fusion.39 = bf16[4,1,2,1024,32]{3,4,2,0,1:T(8,128)(2,1)S(1)} fusion(s32[1024]{0:T(1024)S(1)} %multiply_add_fusion.1, bf16[4,2,1024,32]{2,3,1,0:T(8,128)(2,1)S(1)} %all_to_all.40, pred[1024,32]{0,1:T(8,128)(4,1)S(1)} %iota_compare_fusion), kind=kOutput, calls=%fused_computation.73 | convolution fusion | flops 553123840 | bytes 1085440 | tf_op jit(solution)/shard_map/crslk,tl->crstk/dot_general | solution.py:56
  98.3 6.8 %copy.29 = bf16[6,1,2,1024,32]{4,2,0,1,3:T(2,128)(2,1)S(1)} copy(bf16[6,1,2,1024,32]{3,4,2,0,1:T(8,128)(2,1)} %pad_maximum_fusion.8) | data formatting | bytes 1572864 | tf_op jit(solution)/shard_map/concatenate | solution.py:68
  105.1 3.7 %reshape.1277 = bf16[32,2,6144]{2,1,0:T(2,128)(2,1)} reshape(bf16[1024,1,6,2,32]{4,3,2,1,0:T(2,128)(2,1)S(1)} %bitcast.359) | data formatting | bytes 1572864
  108.8 5.1 %all-to-all-start.1 = ((bf16[32,2,6144]{2,1,0:T(2,128)(2,1)}), bf16[32,2,6144]{2,1,0:T(2,128)(2,1)}, u32[]{:S(2)}, u32[]{:S(2)}) async-start(bf16[32,2,6144]{2,1,0:T(2,128)(2,1)} %reshape.1277), calls=%async_computation.1 | async-start | bytes 1572864 | tf_op jit(solution)/shard_map/all_to_all | solution.py:69
  113.9 9.9 %cosine_convert_fusion.6 = (bf16[1,128,2048]{2,1,0:T(8,128)(2,1)}, bf16[1,128,2048]{2,1,0:T(8,128)(2,1)}, bf16[1,128,2048]{2,1,0:T(8,128)(2,1)}, bf16[1,128,2048]{2,1,0:T(8,128)(2,1)}) fusion(s32[128]{0:T(128)S(1)} %get-tuple-element.19, s32[128]{0:T(128)S(1)} %get-tuple-element.16), kind=kLoop, calls=%fused_computation.169 | loop fusion | flops 8912896 | bytes 2098176 | tf_op jit(solution)/shard_map/convert.28
  123.8 9.9 %cosine_convert_fusion.4 = (bf16[1,128,2048]{2,1,0:T(8,128)(2,1)}, bf16[1,128,2048]{2,1,0:T(8,128)(2,1)}, bf16[1,128,2048]{2,1,0:T(8,128)(2,1)}, bf16[1,128,2048]{2,1,0:T(8,128)(2,1)}) fusion(s32[128]{0:T(128)S(1)} %get-tuple-element.17, s32[128]{0:T(128)S(1)} %get-tuple-element.18), kind=kLoop, calls=%fused_computation.161 | loop fusion | flops 8912896 | bytes 2098176 | tf_op jit(solution)/shard_map/convert.24
  133.7 9.8 %cosine_convert_fusion.2 = (bf16[1,128,2048]{2,1,0:T(8,128)(2,1)}, bf16[1,128,2048]{2,1,0:T(8,128)(2,1)}, bf16[1,128,2048]{2,1,0:T(8,128)(2,1)}, bf16[1,128,2048]{2,1,0:T(8,128)(2,1)}) fusion(s32[128]{0:T(128)S(1)} %get-tuple-element.21, s32[128]{0:T(128)S(1)} %get-tuple-element.20), kind=kLoop, calls=%fused_computation.153 | loop fusion | flops 8912896 | bytes 2098176 | tf_op jit(solution)/shard_map/convert.20
  143.5 9.8 %cosine_convert_fusion = (bf16[1,128,2048]{2,1,0:T(8,128)(2,1)}, bf16[1,128,2048]{2,1,0:T(8,128)(2,1)}, bf16[1,128,2048]{2,1,0:T(8,128)(2,1)}, bf16[1,128,2048]{2,1,0:T(8,128)(2,1)}) fusion(s32[128]{0:T(128)S(1)} %get-tuple-element.22, s32[128]{0:T(128)S(1)} %get-tuple-element.23), kind=kLoop, calls=%fused_computation.145 | loop fusion | flops 8912896 | bytes 2098176 | tf_op jit(solution)/shard_map/convert.16
  153.3 5.1 %all-to-all-done.1 = bf16[32,2,6144]{2,1,0:T(2,128)(2,1)} async-done(((bf16[32,2,6144]{2,1,0:T(2,128)(2,1)}), bf16[32,2,6144]{2,1,0:T(2,128)(2,1)}, u32[]{:S(2)}, u32[]{:S(2)}) %all-to-all-start.1) | async-done | bytes 786464 | tf_op jit(solution)/shard_map/all_to_all | solution.py:69
  158.4 7.2 %reshape.1278 = bf16[1024,1,6,2,32]{4,3,2,1,0:T(2,128)(2,1)S(1)} reshape(bf16[32,2,6144]{2,1,0:T(2,128)(2,1)} %all-to-all-done.1) | data formatting | bytes 1572864
  165.6 3.7 %copy.58 = bf16[6,1,2,32,32,32]{5,3,4,2,0,1:T(8,128)(2,1)} copy(bf16[6,1,2,32,32,32]{5,2,0,4,3,1:T(2,128)(2,1)S(1)} %bitcast.355) | data formatting | bytes 1572864 | tf_op jit(solution)/shard_map/all_to_all | solution.py:69
  169.3 5.3 %all_to_all.44 = bf16[6,1,2,32,1024]{4,3,2,0,1:T(8,128)(2,1)S(1)} reshape(bf16[6,1,2,32,32,32]{5,4,3,2,0,1:T(8,128)(2,1)} %bitcast.356) | data formatting | bytes 1572864 | tf_op jit(solution)/shard_map/all_to_all | solution.py:69
  180.6 3.2 %collective-permute-start.1 = (f32[2,1,32,2048]{3,2,1,0:T(8,128)S(1)}, f32[2,1,32,2048]{3,2,1,0:T(8,128)S(1)}, u32[]{:S(2)}, u32[]{:S(2)}) collective-permute-start(f32[2,1,32,2048]{3,2,1,0:T(8,128)S(1)} %pad_maximum_fusion.25), channel_id=1, source_target_pairs={{0,1},{1,2},{2,3},{3,4},{4,5},{5,6},{6,7},{7,8},{8,9},{9,10},{10,1... | collective-permute-start | bytes 1572872 | tf_op jit(solution)/shard_map/ppermute | solution.py:22
  186.4 4.6 %collective-permute-start.2 = (f32[2,1,32,2048]{3,2,1,0:T(8,128)S(1)}, f32[2,1,32,2048]{3,2,1,0:T(8,128)S(1)}, u32[]{:S(2)}, u32[]{:S(2)}) collective-permute-start(f32[2,1,32,2048]{3,2,1,0:T(8,128)S(1)} %pad_maximum_fusion.26), channel_id=1, source_target_pairs={{0,1},{1,2},{2,3},{3,4},{4,5},{5,6},{6,7},{7,8},{8,9},{9,10},{10,1... | collective-permute-start | bytes 1572872 | tf_op jit(solution)/shard_map/ppermute | solution.py:22
  193.9 3.9 %collective-permute-done = f32[2,1,32,2048]{3,2,1,0:T(8,128)S(1)} collective-permute-done((f32[2,1,32,2048]{3,2,1,0:T(8,128)S(1)}, f32[2,1,32,2048]{3,2,1,0:T(8,128)S(1)}, u32[]{:S(2)}, u32[]{:S(2)}) %collective-permute-start) | collective-permute-done | bytes 524320 | tf_op jit(solution)/shard_map/ppermute | solution.py:24
  198.0 11.0 %collective-permute-done.3 = f32[2,1,32,2048]{3,2,1,0:T(8,128)S(1)} collective-permute-done((f32[2,1,32,2048]{3,2,1,0:T(8,128)S(1)}, f32[2,1,32,2048]{3,2,1,0:T(8,128)S(1)}, u32[]{:S(2)}, u32[]{:S(2)}) %collective-permute-start.3) | collective-permute-done | bytes 524320 | tf_op jit(solution)/shard_map/ppermute | solution.py:24
  214.3 6.8 %copy.31 = bf16[6,1,2,32,1024]{3,2,1,0,4:T(2,128)(2,1)S(1)} copy(bf16[6,1,2,32,1024]{4,3,0,2,1:T(8,128)(2,1)} %multiply_convert_fusion) | data formatting | bytes 1572864 | tf_op jit(solution)/shard_map/convert_element_type | solution.py:110
  221.1 3.7 %reshape.1279 = bf16[32,2,6144]{2,1,0:T(2,128)(2,1)} reshape(bf16[1024,6,1,2,32]{4,3,2,1,0:T(2,128)(2,1)S(1)} %bitcast.360) | data formatting | bytes 1572864
  224.9 9.4 %all-to-all-start.2 = ((bf16[32,2,6144]{2,1,0:T(2,128)(2,1)}), bf16[32,2,6144]{2,1,0:T(2,128)(2,1)}, u32[]{:S(2)}, u32[]{:S(2)}) async-start(bf16[32,2,6144]{2,1,0:T(2,128)(2,1)} %reshape.1279), calls=%async_computation.2 | async-start | bytes 1572864 | tf_op jit(solution)/shard_map/all_to_all | solution.py:112
  234.9 4.6 %reshape.1245 = f32[4,1,2,1024,32]{3,4,2,0,1:T(8,128)} reshape(f32[4,1,2,32,32,32]{4,3,5,2,0,1:T(8,128)} %get-tuple-element.10) | data formatting | bytes 2097152 | tf_op jit(solution)/shard_map/convert_element_type | solution.py:117
  239.5 39.3 %all-to-all-done.2 = bf16[32,2,6144]{2,1,0:T(2,128)(2,1)} async-done(((bf16[32,2,6144]{2,1,0:T(2,128)(2,1)}), bf16[32,2,6144]{2,1,0:T(2,128)(2,1)}, u32[]{:S(2)}, u32[]{:S(2)}) %all-to-all-start.2) | async-done | bytes 786464 | tf_op jit(solution)/shard_map/all_to_all | solution.py:112
  278.8 7.2 %reshape.1280 = bf16[1024,6,1,2,32]{4,3,2,1,0:T(2,128)(2,1)S(1)} reshape(bf16[32,2,6144]{2,1,0:T(2,128)(2,1)} %all-to-all-done.2) | data formatting | bytes 1572864
  286.0 3.7 %copy.57 = bf16[6,1,2,32,32,32]{3,4,5,2,0,1:T(8,128)(2,1)} copy(bf16[6,1,2,32,32,32]{3,2,0,5,4,1:T(2,128)(2,1)S(1)} %bitcast.357) | data formatting | bytes 1572864 | tf_op jit(solution)/shard_map/all_to_all | solution.py:112
  289.6 5.0 %reshape.1244 = bf16[6,2,1024,32]{2,3,1,0:T(8,128)(2,1)S(1)} reshape(bf16[6,1,2,32,32,32]{4,3,5,2,0,1:T(8,128)(2,1)} %bitcast.358) | data formatting | bytes 1572864 | tf_op jit(solution)/shard_map/reshape.39
  294.7 16.2 %fusion.33 = f32[6,2,32,1024]{3,2,1,0:T(8,128)S(1)} fusion(bf16[6,2,1024,32]{2,3,1,0:T(8,128)(2,1)S(1)} %reshape.1244, s32[1024]{0:T(1024)S(1)} %multiply_add_fusion.1, pred[32,1024]{1,0:T(8,128)(4,1)S(1)} %iota_compare_fusion.1), kind=kOutput, calls=%fused_computation.71 | convolution fusion | flops 821428224 | bytes 2396160 | tf_op jit(solution)/shard_map/crstk,tl->crskl/dot_general | solution.py:114
  (84 shorter events, 27.8 us)
Async XLA Ops:
  19.0 20.1 %copy-start.17 = (s32[1024]{0:T(1024)S(1)}, s32[1024]{0:T(1024)}, u32[]{:S(2)}) copy-start(s32[1024]{0:T(1024)} %param.7) | copy-start | bytes 12292
  19.0 20.4 %copy-start.18 = (bf16[2,1,2,32,1024]{4,3,2,1,0:T(8,128)(2,1)S(1)}, bf16[2,1,2,32,1024]{4,3,2,1,0:T(8,128)(2,1)}, u32[]{:S(2)}) copy-start(bf16[2,1,2,32,1024]{4,3,2,1,0:T(8,128)(2,1)} %param.5) | copy-start | bytes 786436
  21.7 50.8 %all-to-all-start = ((bf16[32,2,4096]{2,1,0:T(2,128)(2,1)}), bf16[32,2,4096]{2,1,0:T(2,128)(2,1)S(1)}, u32[]{:S(2)}, u32[]{:S(2)}) async-start(bf16[32,2,4096]{2,1,0:T(2,128)(2,1)} %reshape.1275), calls=%async_computation | async-start | bytes 1048576 | tf_op jit(solution)/shard_map/all_to_all | solution.py:54
  108.8 49.6 %all-to-all-start.1 = ((bf16[32,2,6144]{2,1,0:T(2,128)(2,1)}), bf16[32,2,6144]{2,1,0:T(2,128)(2,1)}, u32[]{:S(2)}, u32[]{:S(2)}) async-start(bf16[32,2,6144]{2,1,0:T(2,128)(2,1)} %reshape.1277), calls=%async_computation.1 | async-start | bytes 1572864 | tf_op jit(solution)/shard_map/all_to_all | solution.py:69
  169.3 5.3 %copy-start.3 = (bf16[1,128,2048]{2,1,0:T(8,128)(2,1)S(1)}, bf16[1,128,2048]{2,1,0:T(8,128)(2,1)}, u32[]{:S(2)}) copy-start(bf16[1,128,2048]{2,1,0:T(8,128)(2,1)} %get-tuple-element.38) | copy-start | bytes 1572868
  169.3 5.4 %copy-start.4 = (bf16[1,128,2048]{2,1,0:T(8,128)(2,1)S(1)}, bf16[1,128,2048]{2,1,0:T(8,128)(2,1)}, u32[]{:S(2)}) copy-start(bf16[1,128,2048]{2,1,0:T(8,128)(2,1)} %get-tuple-element.39) | copy-start | bytes 1572868
  174.6 1.0 copy-start.11
  174.7 1.2 copy-start.12
  174.7 1.6 copy-start.1
  174.7 1.6 copy-start.2
  175.8 1.1 copy-start.9
  175.8 1.3 copy-start.10
  176.3 1.2 copy-start.5
  176.3 1.3 copy-start.6
  177.1 1.1 copy-start.13
  177.1 1.3 copy-start.14
  177.5 1.2 copy-start.7
  177.6 1.3 copy-start.8
  178.4 1.1 copy-start.15
  178.4 1.3 copy-start.16
  180.6 13.3 %collective-permute-start.1 = (f32[2,1,32,2048]{3,2,1,0:T(8,128)S(1)}, f32[2,1,32,2048]{3,2,1,0:T(8,128)S(1)}, u32[]{:S(2)}, u32[]{:S(2)}) collective-permute-start(f32[2,1,32,2048]{3,2,1,0:T(8,128)S(1)} %pad_maximum_fusion.25), channel_id=1, source_target_pairs={{0,1},{1,2},{2,3},{3,4},{4,5},{5,6},{6,7},{7,8},{8,9},{9,10},{10,1... | collective-permute-start | bytes 1572872 | tf_op jit(solution)/shard_map/ppermute | solution.py:22
  183.7 14.0 %collective-permute-start = (f32[2,1,32,2048]{3,2,1,0:T(8,128)S(1)}, f32[2,1,32,2048]{3,2,1,0:T(8,128)S(1)}, u32[]{:S(2)}, u32[]{:S(2)}) collective-permute-start(f32[2,1,32,2048]{3,2,1,0:T(8,128)S(1)} %pad_maximum_fusion.25), channel_id=1, source_target_pairs={{1,0},{2,1},{3,2},{4,3},{5,4},{6,5},{7,6},{8,7},{9,8},{10,9},{11,1... | collective-permute-start | bytes 1572872 | tf_op jit(solution)/shard_map/ppermute | solution.py:24
  185.1 23.9 %collective-permute-start.3 = (f32[2,1,32,2048]{3,2,1,0:T(8,128)S(1)}, f32[2,1,32,2048]{3,2,1,0:T(8,128)S(1)}, u32[]{:S(2)}, u32[]{:S(2)}) collective-permute-start(f32[2,1,32,2048]{3,2,1,0:T(8,128)S(1)} %pad_maximum_fusion.26), channel_id=1, source_target_pairs={{1,0},{2,1},{3,2},{4,3},{5,4},{6,5},{7,6},{8,7},{9,8},{10,9},{11,1... | collective-permute-start | bytes 1572872 | tf_op jit(solution)/shard_map/ppermute | solution.py:24
  186.4 22.6 %collective-permute-start.2 = (f32[2,1,32,2048]{3,2,1,0:T(8,128)S(1)}, f32[2,1,32,2048]{3,2,1,0:T(8,128)S(1)}, u32[]{:S(2)}, u32[]{:S(2)}) collective-permute-start(f32[2,1,32,2048]{3,2,1,0:T(8,128)S(1)} %pad_maximum_fusion.26), channel_id=1, source_target_pairs={{0,1},{1,2},{2,3},{3,4},{4,5},{5,6},{6,7},{7,8},{8,9},{9,10},{10,1... | collective-permute-start | bytes 1572872 | tf_op jit(solution)/shard_map/ppermute | solution.py:22
  224.9 53.9 %all-to-all-start.2 = ((bf16[32,2,6144]{2,1,0:T(2,128)(2,1)}), bf16[32,2,6144]{2,1,0:T(2,128)(2,1)}, u32[]{:S(2)}, u32[]{:S(2)}) async-start(bf16[32,2,6144]{2,1,0:T(2,128)(2,1)} %reshape.1279), calls=%async_computation.2 | async-start | bytes 1572864 | tf_op jit(solution)/shard_map/all_to_all | solution.py:112
  294.7 17.0 %copy-start = (f32[4,1,2,1024,32]{3,4,2,0,1:T(8,128)S(1)}, f32[4,1,2,1024,32]{3,4,2,0,1:T(8,128)}, u32[]{:S(2)}) copy-start(f32[4,1,2,1024,32]{3,4,2,0,1:T(8,128)} %reshape.1245) | copy-start | bytes 3145732
where the time goes:
time: 319 us; the launch traced here: 313 us
  local copies, waits for them, and re-layouts  79.9 us (25%)
  waiting for transfers between devices  79 us (25%)
  matrix products  56.2 us (18%)
  other arithmetic  53.7 us (17%)
  starting transfers between devices  42.2 us (13%)
    another operation x5, other arithmetic  39.4 us
    all_to_all x1, waiting for transfers between devices, local(): lax.all_to_all(spectra, 'ma', split_axis=4, concat_axis=3, tiled=True)  39.3 us
    unnamed x47, local copies, waits for them, and re-layouts  31.5 us
    all_to_all x1, starting transfers between devices, local(): lax.all_to_all(listed, 'ma', split_axis=4, concat_axis=3, tiled=True)  17.4 us
    all_to_all x1, waiting for transfers between devices, local(): lax.all_to_all(listed, 'ma', split_axis=4, concat_axis=3, tiled=True)  16.9 us
    dot_general x1, matrix products, local(): jnp.einsum('crslk,tl->crstk', jnp.where(live_cols, owned_seed, zero_value...  16.3 us
    dot_general x1, matrix products, local(): jnp.einsum('crskl,tl->crstk', jnp.where(live_rows, cotangent, zero_value)...  16.2 us
    dot_general x1, matrix products, local(): jnp.einsum('crstk,tl->crskl', returned, back_table, preferred_element_typ...  16.2 us
  transfers between devices with their start and end apart: 7, of which 6 were waited for; matrix products, arithmetic and copies ran while one was open for 19% of the time, Pallas kernels for 0%

commit v1 on v0

v1 whole, which is shorter than its diff:
```python
import functools
import math

import jax
import jax.numpy as jnp
import numpy as np
from jax import lax
from jax.experimental import pallas as pl
from jax.experimental.pallas import tpu as pltpu
from jax.sharding import PartitionSpec as P

MESH = pl.DeviceIdType.MESH
LANES = 128
OWN = 32
F32 = jnp.float32
BF16 = jnp.bfloat16

NT = (((1,), (1,)), ((), ()))
NN = (((1,), (0,)), ((), ()))


def lat_constant(size):
    phase = (2 * np.arange(size)[:, None] + 1) * np.arange(size)[None, :] % (4 * size)
    return np.cos(phase * (math.pi / (2 * size))).astype(jnp.bfloat16)


def wave_constant(waves, points):
    phase = np.arange(waves)[:, None] * np.arange(points)[None, :] % points
    angles = phase * (2.0 * math.pi / points)
    return np.stack([np.cos(angles), -np.sin(angles)]).astype(jnp.bfloat16)


def dot(a, b, dims):
    return lax.dot_general(a, b, dims, preferred_element_type=F32)


def kernel(
    na,
    nr,
    seed_ref,
    cot_ref,
    step_ref,
    owner_ref,
    lat_hbm,
    wave_hbm,
    non_ref,
    next_ref,
    lat,
    nat,
    table,
    onehot,
    owncol,
    mask,
    coef,
    listed,
    rows,
    grid,
    field,
    fwd_halo,
    back_send,
    back_halo,
    send,
    recv,
    load_sem,
    send_sem,
    recv_sem,
    halo_send_sem,
    halo_recv_sem,
):
    me = lax.axis_index("ma")
    radius = lax.axis_index("row")
    size = na * OWN
    points = 2 * size
    quads = na // 4
    chunk = min(256, size)
    wide = min(512, points)
    scale = 2.0 / size

    has_low = radius > 0
    has_high = radius < nr - 1
    barrier = pltpu.get_barrier_semaphore()

    def greet(step, carry):
        peer = lax.rem(me + step, na)
        pl.semaphore_signal(barrier, inc=1, device_id={"ma": peer}, device_id_type=MESH)
        return carry

    lax.fori_loop(1, na, greet, 0)

    @pl.when(has_low)
    def _():
        pl.semaphore_signal(barrier, inc=1, device_id={"row": radius - 1}, device_id_type=MESH)

    @pl.when(has_high)
    def _():
        pl.semaphore_signal(barrier, inc=1, device_id={"row": radius + 1}, device_id_type=MESH)

    load_wave = pltpu.make_async_copy(wave_hbm, nat, load_sem.at[0])
    load_lat = pltpu.make_async_copy(lat_hbm, lat, load_sem.at[1])
    load_wave.start()
    load_lat.start()

    def own_block(k):
        recv[k, me] = send[k, pl.ds(pl.multiple_of(me * OWN, OWN), OWN), :]

    def scatter(k):
        def one(step, carry):
            peer = lax.rem(me + step, na)
            pltpu.make_async_remote_copy(
                src_ref=send.at[k, pl.ds(pl.multiple_of(peer * OWN, OWN), OWN), :],
                dst_ref=recv.at[k, me],
                send_sem=send_sem.at[k],
                recv_sem=recv_sem.at[k],
                device_id={"ma": peer},
                device_id_type=MESH,
            ).start()
            return carry

        lax.fori_loop(1, na, one, 0)
        own_block(k)

    def arrived(k):
        part = recv.at[k, pl.ds(0, na - 1)]
        pltpu.make_async_copy(part, part, recv_sem.at[k]).wait()

    def sent(k):
        part = send.at[k, pl.ds(0, (na - 1) * OWN), :]
        pltpu.make_async_copy(part, part, send_sem.at[k]).wait()

    def halo_copies(src, dst, base):
        down = pltpu.make_async_remote_copy(
            src_ref=src,
            dst_ref=dst.at[1],
            send_sem=halo_send_sem.at[base],
            recv_sem=halo_recv_sem.at[base + 1],
            device_id={"row": jnp.maximum(radius - 1, 0)},
            device_id_type=MESH,
        )
        up = pltpu.make_async_remote_copy(
            src_ref=src,
            dst_ref=dst.at[0],
            send_sem=halo_send_sem.at[base + 1],
            recv_sem=halo_recv_sem.at[base],
            device_id={"row": jnp.minimum(radius + 1, nr - 1)},
            device_id_type=MESH,
        )
        return down, up

    def halo_start(src, dst, base):
        down, up = halo_copies(src, dst, base)

        @pl.when(has_low)
        def _():
            down.start()

        @pl.when(has_high)
        def _():
            up.start()

        @pl.when(jnp.logical_not(has_low))
        def _():
            dst[0] = jnp.zeros_like(dst[0])

        @pl.when(jnp.logical_not(has_high))
        def _():
            dst[1] = jnp.zeros_like(dst[1])

    def halo_wait(src, dst, base):
        down, up = halo_copies(src, dst, base)

        @pl.when(has_low)
        def _():
            up.wait_recv()

        @pl.when(has_high)
        def _():
            down.wait_recv()

    def halo_sent(src, dst, base):
        down, up = halo_copies(src, dst, base)

        @pl.when(has_low)
        def _():
            down.wait_send()

        @pl.when(has_high)
        def _():
            up.wait_send()

    group = lax.broadcasted_iota(jnp.int32, (OWN, LANES), 1) // OWN
    odd = lax.rem(group, 2) == 1
    high = group >= 2

    def regroup(k, put):
        def one(q, carry):
            x = [recv[k, 4 * q + a].astype(F32) for a in range(4)]
            y = [None] * 4
            for a in (0, 2):
                y[a] = jnp.where(odd, pltpu.roll(x[a + 1], 32, 1), x[a])
                y[a + 1] = jnp.where(odd, x[a + 1], pltpu.roll(x[a], 96, 1))
            z = [None] * 4
            for a in (0, 1):
                z[a] = jnp.where(high, pltpu.roll(y[a + 2], 64, 1), y[a])
                z[a + 2] = jnp.where(high, y[a + 2], pltpu.roll(y[a], 64, 1))
            columns = pl.ds(pl.multiple_of(q * LANES, LANES), LANES)
            for g in range(4):
                put(g, columns, z[g])
            return carry

        lax.fori_loop(0, quads, one, 0)

    def stacked(k, left):
        def one(i, carry):
            at = pl.ds(pl.multiple_of(i * chunk, chunk), chunk)
            send[k, at, :] = dot(left[at, :], coef[...], NT).astype(BF16)
            return carry

        lax.fori_loop(0, size // chunk, one, 0)

    def spread(b, carry):
        at = pl.ds(pl.multiple_of(b * LANES, LANES), LANES)
        column = jnp.transpose(jnp.broadcast_to(owner_ref[0:1, at], (LANES, LANES)))
        owncol[at, :] = column
        lane = lax.broadcasted_iota(jnp.int32, (LANES, LANES), 1)
        for c in range(size // LANES):
            onehot[at, c * LANES : (c + 1) * LANES] = jnp.where(
                column == lane + c * LANES, 1.0, 0.0
            ).astype(BF16)
        return carry

    lax.fori_loop(0, size // LANES, spread, 0)

    for k, first in ((0, 0), (1, 1)):
        for c in range(2):
            for s in range(2):
                g = 2 * c + s
                coef[g * OWN : (g + 1) * OWN, :] = seed_ref[first + 2 * c, s]
        stacked(k, onehot)
        if k == 0:
            pl.semaphore_wait(
                barrier, na - 1 + has_low.astype(jnp.int32) + has_high.astype(jnp.int32)
            )
        scatter(k)

    mine = owncol[pl.ds(pl.multiple_of(me * OWN, OWN), OWN), :]
    for c in range(size // LANES):
        lane = lax.broadcasted_iota(jnp.int32, (OWN, LANES), 1) + c * LANES
        mask[:, c * LANES : (c + 1) * LANES] = jnp.where(lane >= mine, 1.0, 0.0)

    load_lat.wait()
    for c in range(2):
        for s in range(2):
            g = 2 * c + s
            coef[g * OWN : (g + 1) * OWN, :] = jnp.where(
                mask[...] > 0.0, cot_ref[c, s].astype(F32), 0.0
            ).astype(BF16)
    stacked(4, lat)

    load_wave.wait()
    wide_steps = points // wide
    tall_steps = size // chunk

    def permute(i, carry):
        s = i // (wide_steps * tall_steps)
        rest = lax.rem(i, wide_steps * tall_steps)
        columns = pl.ds(pl.multiple_of(lax.rem(rest, wide_steps) * wide, wide), wide)
        top = pl.multiple_of((rest // wide_steps) * chunk, chunk)
        table[s, pl.ds(top, chunk), columns] = dot(
            onehot[pl.ds(top, chunk), :], nat[s, :, columns], NN
        ).astype(BF16)
        return carry

    lax.fori_loop(0, 2 * wide_steps * tall_steps, permute, 0)

    arrived(0)

    def keep_toroidal(g, columns, tile):
        listed[2 * (g // 2), g % 2, :, columns] = tile.astype(BF16)
        coef[g * OWN : (g + 1) * OWN, columns] = jnp.where(
            mask[:, columns] > 0.0, tile, 0.0
        ).astype(BF16)

    regroup(0, keep_toroidal)
    stacked(2, lat)
    scatter(2)

    arrived(1)

    def keep_poloidal(g, columns, tile):
        listed[2 * (g // 2) + 1, g % 2, :, columns] = tile.astype(BF16)
        rows[g * OWN : (g + 1) * OWN, columns] = tile.astype(BF16)

    regroup(1, keep_poloidal)
    halo_start(rows, fwd_halo, 0)
    halo_wait(rows, fwd_halo, 0)
    for g in range(4):
        at = slice(g * OWN, (g + 1) * OWN)
        slope = 0.5 * (fwd_halo[1, at, :].astype(F32) - fwd_halo[0, at, :].astype(F32))
        coef[at, :] = jnp.where(mask[...] > 0.0, slope, 0.0).astype(BF16)
    stacked(3, lat)
    scatter(3)
    scatter(4)

    def into_grid(base):
        def put(g, columns, tile):
            grid[base + g // 2, g % 2, :, columns] = tile.astype(BF16)

        return put

    arrived(2)
    regroup(2, into_grid(0))
    arrived(3)
    regroup(3, into_grid(2))

    def on_grid(first, count, columns):
        left = grid[first : first + count]
        total = None
        for s in range(2):
            part = dot(
                left[:, s].reshape(count * OWN, size), table[s, :, columns], NN
            )
            total = part if total is None else total + part
        total = total * scale
        return [total[c * OWN : (c + 1) * OWN] for c in range(count)]

    def terms(i, carry):
        columns = pl.ds(pl.multiple_of(i * wide, wide), wide)
        vel_tor, mag_tor, vel_pol, mag_pol = on_grid(0, 4, columns)
        for c, value in enumerate((vel_tor, mag_tor, vel_pol, mag_pol)):
            field[c, :, columns] = value
        back_send[0:OWN, columns] = (mag_tor * mag_pol - vel_tor * vel_pol).astype(BF16)
        back_send[OWN : 2 * OWN, columns] = (vel_tor * mag_pol - vel_pol * mag_tor).astype(BF16)
        return carry

    def analyse(k, source):
        def one(i, carry):
            at = pl.ds(pl.multiple_of(i * chunk, chunk), chunk)
            parts = [dot(table[s, at, :], source[...], NT) for s in range(2)]
            send[k, at, :] = (scale * jnp.concatenate(parts, axis=1)).astype(BF16)
            return carry

        lax.fori_loop(0, size // chunk, one, 0)

    lax.fori_loop(0, points // wide, terms, 0)
    analyse(5, back_send)
    scatter(5)

    arrived(4)
    regroup(4, into_grid(4))
    tor_grad = back_halo.at[2]

    def grads(i, carry):
        columns = pl.ds(pl.multiple_of(i * wide, wide), wide)
        adj_vel, adj_mag = on_grid(4, 2, columns)
        vel_tor, mag_tor, vel_pol, mag_pol = (field[c, :, columns] for c in range(4))
        back_send[0:OWN, columns] = (-vel_tor * adj_vel - mag_tor * adj_mag).astype(BF16)
        back_send[OWN : 2 * OWN, columns] = (mag_tor * adj_vel + vel_tor * adj_mag).astype(BF16)
        tor_grad[0:OWN, columns] = (-vel_pol * adj_vel + mag_pol * adj_mag).astype(BF16)
        tor_grad[OWN : 2 * OWN, columns] = (mag_pol * adj_vel - vel_pol * adj_mag).astype(BF16)
        return carry

    lax.fori_loop(0, points // wide, grads, 0)
    halo_start(back_send, back_halo, 2)
    analyse(6, tor_grad)
    scatter(6)
    halo_wait(back_send, back_halo, 2)
    tor_grad[...] = (
        0.5 * (back_halo[0].astype(F32) - back_halo[1].astype(F32))
    ).astype(BF16)
    analyse(7, tor_grad)
    scatter(7)

    step = step_ref[0]

    def finish(k, put):
        arrived(k)

        def keep(g, columns, tile):
            rows[g * OWN : (g + 1) * OWN, columns] = tile.astype(BF16)

        if k == 5:
            halo_sent(rows, fwd_halo, 0)
        regroup(k, keep)

        def one(i, carry):
            columns = pl.ds(pl.multiple_of(i * chunk, chunk), chunk)
            result = dot(rows[...], lat[:, columns], NN)
            live = mask[:, columns] > 0.0
            for g in range(4):
                put(
                    g // 2,
                    g % 2,
                    columns,
                    jnp.where(live, result[g * OWN : (g + 1) * OWN], 0.0),
                )
            return carry

        lax.fori_loop(0, size // chunk, one, 0)

    def put_term(s, c, columns, value):
        non_ref[c, s, :, columns] = value

    def put_seed(first):
        def put(s, c, columns, value):
            channel = 2 * c + first
            next_ref[channel, s, :, columns] = (
                listed[channel, s, :, columns].astype(F32) - step * value
            )

        return put

    finish(5, put_term)
    finish(6, put_seed(0))
    finish(7, put_seed(1))
    halo_sent(back_send, back_halo, 2)
    for k in range(8):
        sent(k)


def local(lat_table, wave_table, seed_field, cotangent, step_size, owner_list):
    na = lax.axis_size("ma")
    nr = lax.axis_size("row")
    size = na * OWN
    points = 2 * size
    vmem = pl.BlockSpec(memory_space=pltpu.VMEM)
    hbm = pl.BlockSpec(memory_space=pl.ANY)
    nonlinear, seed_next = pl.pallas_call(
        functools.partial(kernel, na, nr),
        out_shape=(
            jax.ShapeDtypeStruct((2, 2, OWN, size), F32),
            jax.ShapeDtypeStruct((4, 2, OWN, size), F32),
        ),
        in_specs=[vmem, vmem, pl.BlockSpec(memory_space=pltpu.SMEM), vmem, hbm, hbm],
        out_specs=(vmem, vmem),
        scratch_shapes=[
            pltpu.VMEM((size, size), BF16),
            pltpu.VMEM((2, size, points), BF16),
            pltpu.VMEM((2, size, points), BF16),
            pltpu.VMEM((size, size), BF16),
            pltpu.VMEM((size, LANES), jnp.int32),
            pltpu.VMEM((OWN, size), F32),
            pltpu.VMEM((4 * OWN, size), BF16),
            pltpu.VMEM((4, 2, OWN, size), BF16),
            pltpu.VMEM((4 * OWN, size), BF16),
            pltpu.VMEM((6, 2, OWN, size), BF16),
            pltpu.VMEM((4, OWN, points), F32),
            pltpu.VMEM((2, 4 * OWN, size), BF16),
            pltpu.VMEM((2 * OWN, points), BF16),
            pltpu.VMEM((3, 2 * OWN, points), BF16),
            pltpu.VMEM((8, size, LANES), BF16),
            pltpu.VMEM((8, na, OWN, LANES), BF16),
            pltpu.SemaphoreType.DMA((2,)),
            pltpu.SemaphoreType.DMA((8,)),
            pltpu.SemaphoreType.DMA((8,)),
            pltpu.SemaphoreType.DMA((4,)),
            pltpu.SemaphoreType.DMA((4,)),
        ],
        compiler_params=pltpu.CompilerParams(
            collective_id=0, has_side_effects=True, vmem_limit_bytes=56 << 20
        ),
    )(
        seed_field.reshape(4, 2, OWN, size),
        cotangent.reshape(2, 2, OWN, size),
        step_size,
        owner_list.reshape(1, size),
        lat_table,
        wave_table,
    )
    return (
        nonlinear.reshape(2, 1, 2, OWN, size),
        seed_next.reshape(4, 1, 2, OWN, size),
    )


def solution(mesh):
    split = P(None, "row", None, "ma", None)
    size = mesh.shape["ma"] * OWN
    lat_table = lat_constant(size)
    wave_table = wave_constant(size, 2 * size)
    body = jax.shard_map(
        local,
        mesh=mesh,
        in_specs=(P(), P(), split, split, P(), P()),
        out_specs=(split, split),
        check_vma=False,
    )

    def run(seed_field, cotangent, step_size, owner_list):
        return body(
            jnp.asarray(lat_table), jnp.asarray(wave_table), seed_field, cotangent, step_size, owner_list
        )

    return run
```

time: 319 us -> 125 us (0.39); the launches traced: 313 us -> 123 us
  Pallas kernels: 0 us -> 117 us
  waiting for transfers between devices: 79 us -> 0 us
  local copies, waits for them, and re-layouts: 79.9 us -> 4.19 us
  matrix products: 56.2 us -> 0 us
  other arithmetic: 53.7 us -> 0 us
  starting transfers between devices: 42.2 us -> 0 us
    pallas_call x0 -> x1, Pallas kernels: none -> 117 us  [local(): pl.pallas_call(functools.partial(kernel, na, nr), out_shape=(jax.ShapeDty...]
    all_to_all x3 -> x0, waiting for transfers between devices: 61.3 us -> none  [the longest x1 39.3 us: local(): lax.all_to_all(spectra, 'ma', split_axis=4, concat_axis=3, tiled=True)]
    dot_general x19 -> x0, matrix products: 56.2 us -> none  [the longest x1 16.3 us: local(): jnp.einsum('crslk,tl->crstk', jnp.where(live_cols, owned_seed, zero_value...]
    another operation x7 -> x0, other arithmetic: 39.5 us -> none
    all_to_all x3 -> x0, starting transfers between devices: 31.9 us -> none  [the longest x1 17.4 us: local(): lax.all_to_all(listed, 'ma', split_axis=4, concat_axis=3, tiled=True)]
    unnamed x47 -> x2, local copies, waits for them, and re-layouts: 31.5 us -> 4.19 us
    ppermute x4 -> x0, waiting for transfers between devices: 17.7 us -> none  [the longest x2 14.8 us: with_halo(): lax.ppermute(head, axis, [((i + 1) % count, i) for i in range(ends)])]
    all_to_all x4 -> x0, local copies, waits for them, and re-layouts: 16.2 us -> none  [the longest x2 9 us: local(): lax.all_to_all(spec_rows, 'ma', split_axis=3, concat_axis=4, tiled=True)]
  transfers between devices with their start and end apart: 7 -> 0, of which waited for: 6 -> 0; matrix products, arithmetic and copies ran while one was open for 19% -> 0% of each run, Pallas kernels for 0% -> 0%
where the time goes in v1:
time: 125 us; the launch traced here: 123 us
  Pallas kernels  117 us (94%)
  local copies, waits for them, and re-layouts  4.19 us (3%)
  between operations  1.28 us (1%)
    pallas_call x1, Pallas kernels, local(): pl.pallas_call(functools.partial(kernel, na, nr), out_shape=(jax.ShapeDty...  117 us
    unnamed x2, local copies, waits for them, and re-layouts  4.19 us

profile of v1, /device:TPU:1, one launch (start us, length us, event | category | flops | bytes accessed | tf_op | source)
XLA Modules:
  0.0 122.9 jit_solution(2577036748899320553)
XLA Ops:
  1.3 117.4 %shard_map.77 = (f32[2,2,32,1024]{3,2,1,0:T(8,128)}, f32[4,2,32,1024]{3,2,1,0:T(8,128)}) custom-call(bf16[4,2,32,1024]{3,2,1,0:T(8,128)(2,1)} %bitcast.11, bf16[2,2,32,1024]{3,2,1,0:T(8,128)(2,1)} %bitcast.12, f32[1]{0:T(128)S(6)} %copy.12.step_ref, s32[1,1024]{1,0:T(1,128)} %bitcast.13, bf16[1024,1024]{1,0:T(8,128)(2,1)} %constant.4.clone.lat_hbm, ...), custom_call_target="tpu_custom_call" | custom-call | tf_op jit(solution)/shard_map/pallas_call | solution.py:427
  118.7 1.9 %copy.13 = f32[2,1,2,32,1024]{4,3,2,1,0:T(8,128)} copy(f32[2,1,2,32,1024]{4,3,2,1,0:T(8,128)} %bitcast.10) | data formatting | bytes 1048576
  120.6 2.3 %copy.14 = f32[4,1,2,32,1024]{4,3,2,1,0:T(8,128)} copy(f32[4,1,2,32,1024]{4,3,2,1,0:T(8,128)} %bitcast.9) | data formatting | bytes 2097152

commit v2 on v1

--- a/solution.py
+++ b/solution.py
@@ -37,12 +37,18 @@
 def kernel(
     na,
     nr,
+    seed_hbm,
+    cot_hbm,
+    step_hbm,
+    owner_hbm,
+    lat_hbm,
+    wave_hbm,
+    non_hbm,
+    next_hbm,
     seed_ref,
     cot_ref,
     step_ref,
     owner_ref,
-    lat_hbm,
-    wave_hbm,
     non_ref,
     next_ref,
     lat,
@@ -62,6 +68,7 @@
     send,
     recv,
     load_sem,
+    store_sem,
     send_sem,
     recv_sem,
     halo_send_sem,
@@ -73,12 +80,30 @@
     points = 2 * size
     quads = na // 4
     chunk = min(256, size)
-    wide = min(512, points)
+    tall = min(512, size)
+    wide = min(1024, points)
     scale = 2.0 / size
 
     has_low = radius > 0
     has_high = radius < nr - 1
     barrier = pltpu.get_barrier_semaphore()
+
+    loads = [
+        pltpu.make_async_copy(src, dst, load_sem.at[i])
+        for i, (src, dst) in enumerate(
+            (
+                (owner_hbm, owner_ref),
+                (seed_hbm, seed_ref),
+                (lat_hbm, lat),
+                (cot_hbm, cot_ref),
+                (step_hbm, step_ref),
+                (wave_hbm, nat),
+            )
+        )
+    ]
+    load_owner, load_seed, load_lat, load_cot, load_step, load_wave = loads
+    for load in loads:
+        load.start()
 
     def greet(step, carry):
         peer = lax.rem(me + step, na)
@@ -95,29 +120,43 @@
     def _():
         pl.semaphore_signal(barrier, inc=1, device_id={"row": radius + 1}, device_id_type=MESH)
 
-    load_wave = pltpu.make_async_copy(wave_hbm, nat, load_sem.at[0])
-    load_lat = pltpu.make_async_copy(lat_hbm, lat, load_sem.at[1])
-    load_wave.start()
-    load_lat.start()
-
-    def own_block(k):
-        recv[k, me] = send[k, pl.ds(pl.multiple_of(me * OWN, OWN), OWN), :]
-
-    def scatter(k):
-        def one(step, carry):
-            peer = lax.rem(me + step, na)
-            pltpu.make_async_remote_copy(
-                src_ref=send.at[k, pl.ds(pl.multiple_of(peer * OWN, OWN), OWN), :],
-                dst_ref=recv.at[k, me],
-                send_sem=send_sem.at[k],
-                recv_sem=recv_sem.at[k],
-                device_id={"ma": peer},
-                device_id_type=MESH,
-            ).start()
+    def scatter(k, first, count):
+        def one(i, carry):
+            peer = first + i
+            block = send.at[k, pl.ds(pl.multiple_of(peer * OWN, OWN), OWN), :]
+
+            @pl.when(peer != me)
+            def _():
+                pltpu.make_async_remote_copy(
+                    src_ref=block,
+                    dst_ref=recv.at[k, me],
+                    send_sem=send_sem.at[k],
+                    recv_sem=recv_sem.at[k],
+                    device_id={"ma": peer},
+                    device_id_type=MESH,
+                ).start()
+
+            @pl.when(peer == me)
+            def _():
+                recv[k, me] = block[...]
+
             return carry
 
-        lax.fori_loop(1, na, one, 0)
-        own_block(k)
+        lax.fori_loop(0, count, one, 0)
+
+    def in_turn(k, height, rows_of, go=True):
+        count = size // height
+        peers = height // OWN
+
+        def one(i, carry):
+            turn = lax.rem(me // peers + i, count)
+            at = pl.ds(pl.multiple_of(turn * height, height), height)
+            send[k, at, :] = rows_of(at).astype(BF16)
+            if go:
+                scatter(k, turn * peers, peers)
+            return carry
+
+        lax.fori_loop(0, count, one, 0)
 
     def arrived(k):
         part = recv.at[k, pl.ds(0, na - 1)]
@@ -147,15 +186,23 @@
         return down, up
 
     def halo_start(src, dst, base):
-        down, up = halo_copies(src, dst, base)
-
-        @pl.when(has_low)
-        def _():
-            down.start()
-
-        @pl.when(has_high)
-        def _():
-            up.start()
+        height = src.shape[0] // 4
+
+        def piece(i, carry):
+            at = pl.ds(pl.multiple_of(i * height, height), height)
+            down, up = halo_copies(src.at[at], dst.at[:, at], base)
+
+            @pl.when(has_low)
+            def _():
+                down.start()
+
+            @pl.when(has_high)
+            def _():
+                up.start()
+
+            return carry
+
+        lax.fori_loop(0, 4, piece, 0)
 
         @pl.when(jnp.logical_not(has_low))
         def _():
@@ -207,15 +254,12 @@
                 put(g, columns, z[g])
             return carry
 
-        lax.fori_loop(0, quads, one, 0)
-
-    def stacked(k, left):
-        def one(i, carry):
-            at = pl.ds(pl.multiple_of(i * chunk, chunk), chunk)
-            send[k, at, :] = dot(left[at, :], coef[...], NT).astype(BF16)
-            return carry
-
-        lax.fori_loop(0, size // chunk, one, 0)
+        lax.fori_loop(0, quads, one, 0, unroll=min(4, quads))
+
+    def stacked(k, left, height, go=True):
+        in_turn(k, height, lambda at: dot(left[at, :], coef[...], NT), go)
+
+    load_owner.wait()
 
     def spread(b, carry):
         at = pl.ds(pl.multiple_of(b * LANES, LANES), LANES)
@@ -230,17 +274,14 @@
 
     lax.fori_loop(0, size // LANES, spread, 0)
 
-    for k, first in ((0, 0), (1, 1)):
+    load_seed.wait()
+    pl.semaphore_wait(barrier, na - 1 + has_low.astype(jnp.int32) + has_high.astype(jnp.int32))
+    for k in range(2):
         for c in range(2):
             for s in range(2):
                 g = 2 * c + s
-                coef[g * OWN : (g + 1) * OWN, :] = seed_ref[first + 2 * c, s]
-        stacked(k, onehot)
-        if k == 0:
-            pl.semaphore_wait(
-                barrier, na - 1 + has_low.astype(jnp.int32) + has_high.astype(jnp.int32)
-            )
-        scatter(k)
+                coef[g * OWN : (g + 1) * OWN, :] = seed_ref[k + 2 * c, s]
+        stacked(k, onehot, chunk)
 
     mine = owncol[pl.ds(pl.multiple_of(me * OWN, OWN), OWN), :]
     for c in range(size // LANES):
@@ -248,25 +289,28 @@
         mask[:, c * LANES : (c + 1) * LANES] = jnp.where(lane >= mine, 1.0, 0.0)
 
     load_lat.wait()
+    load_cot.wait()
+    load_step.wait()
     for c in range(2):
         for s in range(2):
             g = 2 * c + s
             coef[g * OWN : (g + 1) * OWN, :] = jnp.where(
                 mask[...] > 0.0, cot_ref[c, s].astype(F32), 0.0
             ).astype(BF16)
-    stacked(4, lat)
+    stacked(4, lat, tall, go=False)
 
     load_wave.wait()
-    wide_steps = points // wide
-    tall_steps = size // chunk
+    part = min(512, points)
+    wide_steps = points // part
+    tall_steps = size // tall
 
     def permute(i, carry):
         s = i // (wide_steps * tall_steps)
         rest = lax.rem(i, wide_steps * tall_steps)
-        columns = pl.ds(pl.multiple_of(lax.rem(rest, wide_steps) * wide, wide), wide)
-        top = pl.multiple_of((rest // wide_steps) * chunk, chunk)
-        table[s, pl.ds(top, chunk), columns] = dot(
-            onehot[pl.ds(top, chunk), :], nat[s, :, columns], NN
+        columns = pl.ds(pl.multiple_of(lax.rem(rest, wide_steps) * part, part), part)
+        top = pl.multiple_of((rest // wide_steps) * tall, tall)
+        table[s, pl.ds(top, tall), columns] = dot(
+            onehot[pl.ds(top, tall), :], nat[s, :, columns], NN
         ).astype(BF16)
         return carry
 
@@ -281,8 +325,7 @@
         ).astype(BF16)
 
     regroup(0, keep_toroidal)
-    stacked(2, lat)
-    scatter(2)
+    stacked(2, lat, chunk)
 
     arrived(1)
 
@@ -297,9 +340,8 @@
         at = slice(g * OWN, (g + 1) * OWN)
         slope = 0.5 * (fwd_halo[1, at, :].astype(F32) - fwd_halo[0, at, :].astype(F32))
         coef[at, :] = jnp.where(mask[...] > 0.0, slope, 0.0).astype(BF16)
-    stacked(3, lat)
-    scatter(3)
-    scatter(4)
+    stacked(3, lat, chunk)
+    scatter(4, 0, na)
 
     def into_grid(base):
         def put(g, columns, tile):
@@ -333,17 +375,14 @@
         return carry
 
     def analyse(k, source):
-        def one(i, carry):
-            at = pl.ds(pl.multiple_of(i * chunk, chunk), chunk)
+        def made(at):
             parts = [dot(table[s, at, :], source[...], NT) for s in range(2)]
-            send[k, at, :] = (scale * jnp.concatenate(parts, axis=1)).astype(BF16)
-            return carry
-
-        lax.fori_loop(0, size // chunk, one, 0)
+            return scale * jnp.concatenate(parts, axis=1)
+
+        in_turn(k, tall, made)
 
     lax.fori_loop(0, points // wide, terms, 0)
     analyse(5, back_send)
-    scatter(5)
 
     arrived(4)
     regroup(4, into_grid(4))
@@ -362,15 +401,13 @@
     lax.fori_loop(0, points // wide, grads, 0)
     halo_start(back_send, back_halo, 2)
     analyse(6, tor_grad)
-    scatter(6)
     halo_wait(back_send, back_halo, 2)
     tor_grad[...] = (
         0.5 * (back_halo[0].astype(F32) - back_halo[1].astype(F32))
     ).astype(BF16)
     analyse(7, tor_grad)
-    scatter(7)
-
-    step = step_ref[0]
+
+    step = jnp.broadcast_to(step_ref[...].reshape(1, 1), (OWN, chunk))
 
     def finish(k, put):
         arrived(k)
@@ -409,12 +446,38 @@
 
         return put
 
+    stores = [pltpu.make_async_copy(non_ref, non_hbm, store_sem.at[0])]
+    for channel in range(4):
+        stores.append(
+            pltpu.make_async_copy(
+                next_ref.at[channel], next_hbm.at[channel], store_sem.at[channel + 1]
+            )
+        )
     finish(5, put_term)
+    stores[0].start()
     finish(6, put_seed(0))
+    stores[1].start()
+    stores[3].start()
     finish(7, put_seed(1))
+    stores[2].start()
+    stores[4].start()
     halo_sent(back_send, back_halo, 2)
     for k in range(8):
         sent(k)
+    for store in stores:
+        store.wait()
+
+
+def settle(non_in, next_in, non_out, next_out, sem):
+    copies = [pltpu.make_async_copy(non_in, non_out, sem.at[0])]
+    for channel in range(4):
+        copies.append(
+            pltpu.make_async_copy(next_in.at[channel], next_out.at[channel], sem.at[channel + 1])
+        )
+    for copy in copies:
+        copy.start()
+    for copy in copies:
+        copy.wait()
 
 
 def local(lat_table, wave_table, seed_field, cotangent, step_size, owner_list):
@@ -422,17 +485,23 @@
     nr = lax.axis_size("row")
     size = na * OWN
     points = 2 * size
-    vmem = pl.BlockSpec(memory_space=pltpu.VMEM)
     hbm = pl.BlockSpec(memory_space=pl.ANY)
-    nonlinear, seed_next = pl.pallas_call(
+    shapes = (
+        jax.ShapeDtypeStruct((2, 2, OWN, size), F32),
+        jax.ShapeDtypeStruct((4, 2, OWN, size), F32),
+    )
+    outputs = pl.pallas_call(
         functools.partial(kernel, na, nr),
-        out_shape=(
-            jax.ShapeDtypeStruct((2, 2, OWN, size), F32),
-            jax.ShapeDtypeStruct((4, 2, OWN, size), F32),
-        ),
-        in_specs=[vmem, vmem, pl.BlockSpec(memory_space=pltpu.SMEM), vmem, hbm, hbm],
-        out_specs=(vmem, vmem),
+        out_shape=shapes,
+        in_specs=[pl.BlockSpec(memory_space=pltpu.HBM)] * 6,
+        out_specs=(hbm, hbm),
         scratch_shapes=[
+            pltpu.VMEM((4, 2, OWN, size), BF16),
+            pltpu.VMEM((2, 2, OWN, size), BF16),
+            pltpu.VMEM((1,), F32),
+            pltpu.VMEM((1, size), jnp.int32),
+            pltpu.VMEM((2, 2, OWN, size), F32),
+            pltpu.VMEM((4, 2, OWN, size), F32),
             pltpu.VMEM((size, size), BF16),
             pltpu.VMEM((2, size, points), BF16),
             pltpu.VMEM((2, size, points), BF16),
@@ -449,7 +518,8 @@
             pltpu.VMEM((3, 2 * OWN, points), BF16),
             pltpu.VMEM((8, size, LANES), BF16),
             pltpu.VMEM((8, na, OWN, LANES), BF16),
-            pltpu.SemaphoreType.DMA((2,)),
+            pltpu.SemaphoreType.DMA((6,)),
+            pltpu.SemaphoreType.DMA((5,)),
             pltpu.SemaphoreType.DMA((8,)),
             pltpu.SemaphoreType.DMA((8,)),
             pltpu.SemaphoreType.DMA((4,)),
@@ -466,6 +536,14 @@
         lat_table,
         wave_table,
     )
+    nonlinear, seed_next = pl.pallas_call(
+        settle,
+        out_shape=shapes,
+        in_specs=[hbm] * 2,
+        out_specs=(hbm, hbm),
+        scratch_shapes=[pltpu.SemaphoreType.DMA((5,))],
+        compiler_params=pltpu.CompilerParams(vmem_limit_bytes=56 << 20),
+    )(*outputs)
     return (
         nonlinear.reshape(2, 1, 2, OWN, size),
         seed_next.reshape(4, 1, 2, OWN, size),

time: 125 us -> 164 us (1.31)
  Pallas kernels: 117 us -> 161 us
  local copies, waits for them, and re-layouts: 4.19 us -> 0 us
    pallas_call x1 -> x2, Pallas kernels: 117 us -> 161 us  [the longest x1 113 us: local(): pl.pallas_call(functools.partial(kernel, na, nr), out_shape=shapes, in_sp...]
    unnamed x2 -> x0, local copies, waits for them, and re-layouts: 4.19 us -> none
where the time goes in v2:
time: 164 us; the launch traced here: 163 us
  Pallas kernels  161 us (98%)
    pallas_call x1, Pallas kernels, local(): pl.pallas_call(functools.partial(kernel, na, nr), out_shape=shapes, in_sp...  113 us
    pallas_call x1, Pallas kernels, local(): pl.pallas_call(settle, out_shape=shapes, in_specs=[hbm] * 2, out_specs=(h...  48.8 us

profile of v2, /device:TPU:1, one launch (start us, length us, event | category | flops | bytes accessed | tf_op | source)
XLA Modules:
  0.0 162.8 jit_solution(11439446258489225410)
XLA Ops:
  1.3 112.7 %shard_map.77 = (f32[2,2,32,1024]{3,2,1,0:T(8,128)}, f32[4,2,32,1024]{3,2,1,0:T(8,128)}) custom-call(bf16[4,2,32,1024]{3,2,1,0:T(8,128)(2,1)} %bitcast.9, bf16[2,2,32,1024]{3,2,1,0:T(8,128)(2,1)} %bitcast.10, f32[1]{0:T(128)S(6)} %copy.10.step_hbm, s32[1,1024]{1,0:T(1,128)} %bitcast.11, bf16[1024,1024]{1,0:T(8,128)(2,1)} %constant.4.clone.lat_hbm, ...), custom_call_target="tpu_custom_call" | custom-call | tf_op jit(solution)/shard_map/pallas_call | solution.py:493
  114.0 48.8 %shard_map.78 = (f32[2,2,32,1024]{3,2,1,0:T(8,128)}, f32[4,2,32,1024]{3,2,1,0:T(8,128)}) custom-call(f32[2,2,32,1024]{3,2,1,0:T(8,128)} %get-tuple-element.6.non_in, f32[4,2,32,1024]{3,2,1,0:T(8,128)} %get-tuple-element.7.next_in), custom_call_target="tpu_custom_call" | custom-call | tf_op jit(solution)/shard_map/pallas_call | solution.py:539

commit v3 on v2

--- a/solution.py
+++ b/solution.py
@@ -43,14 +43,12 @@
     owner_hbm,
     lat_hbm,
     wave_hbm,
-    non_hbm,
-    next_hbm,
+    non_ref,
+    next_ref,
     seed_ref,
     cot_ref,
     step_ref,
     owner_ref,
-    non_ref,
-    next_ref,
     lat,
     nat,
     table,
@@ -68,7 +66,6 @@
     send,
     recv,
     load_sem,
-    store_sem,
     send_sem,
     recv_sem,
     halo_send_sem,
@@ -446,38 +443,26 @@
 
         return put
 
-    stores = [pltpu.make_async_copy(non_ref, non_hbm, store_sem.at[0])]
+    finish(5, put_term)
+    finish(6, put_seed(0))
+    finish(7, put_seed(1))
+    halo_sent(back_send, back_halo, 2)
+    for k in range(8):
+        sent(k)
+
+
+def settle(non_in, next_in, non_out, next_out, store_sem):
+    stores = [pltpu.make_async_copy(non_in, non_out, store_sem.at[0])]
     for channel in range(4):
         stores.append(
             pltpu.make_async_copy(
-                next_ref.at[channel], next_hbm.at[channel], store_sem.at[channel + 1]
+                next_in.at[channel], next_out.at[channel], store_sem.at[channel + 1]
             )
         )
-    finish(5, put_term)
-    stores[0].start()
-    finish(6, put_seed(0))
-    stores[1].start()
-    stores[3].start()
-    finish(7, put_seed(1))
-    stores[2].start()
-    stores[4].start()
-    halo_sent(back_send, back_halo, 2)
-    for k in range(8):
-        sent(k)
+    for store in stores:
+        store.start()
     for store in stores:
         store.wait()
-
-
-def settle(non_in, next_in, non_out, next_out, sem):
-    copies = [pltpu.make_async_copy(non_in, non_out, sem.at[0])]
-    for channel in range(4):
-        copies.append(
-            pltpu.make_async_copy(next_in.at[channel], next_out.at[channel], sem.at[channel + 1])
-        )
-    for copy in copies:
-        copy.start()
-    for copy in copies:
-        copy.wait()
 
 
 def local(lat_table, wave_table, seed_field, cotangent, step_size, owner_list):
@@ -492,16 +477,14 @@
     )
     outputs = pl.pallas_call(
         functools.partial(kernel, na, nr),
-        out_shape=shapes,
+        out_shape=(pltpu.VMEM(shapes[0].shape, F32), pltpu.VMEM(shapes[1].shape, F32)),
         in_specs=[pl.BlockSpec(memory_space=pltpu.HBM)] * 6,
-        out_specs=(hbm, hbm),
+        out_specs=(pl.BlockSpec(memory_space=pltpu.VMEM),) * 2,
         scratch_shapes=[
             pltpu.VMEM((4, 2, OWN, size), BF16),
             pltpu.VMEM((2, 2, OWN, size), BF16),
             pltpu.VMEM((1,), F32),
             pltpu.VMEM((1, size), jnp.int32),
-            pltpu.VMEM((2, 2, OWN, size), F32),
-            pltpu.VMEM((4, 2, OWN, size), F32),
             pltpu.VMEM((size, size), BF16),
             pltpu.VMEM((2, size, points), BF16),
             pltpu.VMEM((2, size, points), BF16),
@@ -519,7 +502,6 @@
             pltpu.VMEM((8, size, LANES), BF16),
             pltpu.VMEM((8, na, OWN, LANES), BF16),
             pltpu.SemaphoreType.DMA((6,)),
-            pltpu.SemaphoreType.DMA((5,)),
             pltpu.SemaphoreType.DMA((8,)),
             pltpu.SemaphoreType.DMA((8,)),
             pltpu.SemaphoreType.DMA((4,)),
@@ -541,8 +523,10 @@
         out_shape=shapes,
         in_specs=[hbm] * 2,
         out_specs=(hbm, hbm),
-        scratch_shapes=[pltpu.SemaphoreType.DMA((5,))],
-        compiler_params=pltpu.CompilerParams(vmem_limit_bytes=56 << 20),
+        scratch_shapes=[
+            pltpu.SemaphoreType.DMA((5,)),
+        ],
+        compiler_params=pltpu.CompilerParams(vmem_limit_bytes=40 << 20),
     )(*outputs)
     return (
         nonlinear.reshape(2, 1, 2, OWN, size),

time: 164 us -> 116 us (0.71)
  Pallas kernels: 161 us -> 113 us
    pallas_call x1, Pallas kernels: 48.8 us -> 1.18 us  [local(): pl.pallas_call(settle, out_shape=shapes, in_specs=[hbm] * 2, out_specs=(h...]
where the time goes in v3:
time: 116 us; the launch traced here: 114 us
  Pallas kernels  113 us (97%)
  between operations  1.28 us (1%)
    pallas_call x1, Pallas kernels, local(): pl.pallas_call(functools.partial(kernel, na, nr), out_shape=(pltpu.VMEM(s...  112 us

profile of v3, /device:TPU:1, one launch (start us, length us, event | category | flops | bytes accessed | tf_op | source)
XLA Modules:
  0.0 114.3 jit_solution(10101519012965149061)
XLA Ops:
  1.3 111.9 %shard_map.77 = (f32[2,2,32,1024]{3,2,1,0:T(8,128)S(1)}, f32[4,2,32,1024]{3,2,1,0:T(8,128)S(1)}) custom-call(bf16[4,2,32,1024]{3,2,1,0:T(8,128)(2,1)} %bitcast.9, bf16[2,2,32,1024]{3,2,1,0:T(8,128)(2,1)} %bitcast.10, f32[1]{0:T(128)S(6)} %copy.10.step_hbm, s32[1,1024]{1,0:T(1,128)} %bitcast.11, bf16[1024,1024]{1,0:T(8,128)(2,1)} %constant.4.clone.lat_hbm, ...), custom_call_target="tpu_custom_call" | custom-call | tf_op jit(solution)/shard_map/pallas_call | solution.py:478
  113.1 1.2 %shard_map.78 = (f32[2,2,32,1024]{3,2,1,0:T(8,128)}, f32[4,2,32,1024]{3,2,1,0:T(8,128)}) custom-call(f32[2,2,32,1024]{3,2,1,0:T(8,128)S(1)} %get-tuple-element.6.non_in, f32[4,2,32,1024]{3,2,1,0:T(8,128)S(1)} %get-tuple-element.7.next_in), custom_call_target="tpu_custom_call" | custom-call | tf_op jit(solution)/shard_map/pallas_call | solution.py:521

commit v4 on v3

--- a/solution.py
+++ b/solution.py
@@ -99,8 +99,8 @@
         )
     ]
     load_owner, load_seed, load_lat, load_cot, load_step, load_wave = loads
-    for load in loads:
-        load.start()
+    load_owner.start()
+    load_seed.start()
 
     def greet(step, carry):
         peer = lax.rem(me + step, na)
@@ -116,6 +116,9 @@
     @pl.when(has_high)
     def _():
         pl.semaphore_signal(barrier, inc=1, device_id={"row": radius + 1}, device_id_type=MESH)
+
+    for load in loads[2:]:
+        load.start()
 
     def scatter(k, first, count):
         def one(i, carry):
@@ -137,6 +140,21 @@
             def _():
                 recv[k, me] = block[...]
 
+            return carry
+
+        lax.fori_loop(0, count, one, 0)
+
+    def ahead(k, first, count):
+        def one(i, carry):
+            peer = lax.rem(me + first + i, na)
+            pltpu.make_async_remote_copy(
+                src_ref=send.at[k, pl.ds(pl.multiple_of(peer * OWN, OWN), OWN), :],
+                dst_ref=recv.at[k, me],
+                send_sem=send_sem.at[k],
+                recv_sem=recv_sem.at[k],
+                device_id={"ma": peer},
+                device_id_type=MESH,
+            ).start()
             return carry
 
         lax.fori_loop(0, count, one, 0)
@@ -256,29 +274,35 @@
     def stacked(k, left, height, go=True):
         in_turn(k, height, lambda at: dot(left[at, :], coef[...], NT), go)
 
+    def order(at):
+        for b in range(at.size // LANES):
+            block = pl.ds(pl.multiple_of(at.start + b * LANES, LANES), LANES)
+            column = jnp.transpose(jnp.broadcast_to(owner_ref[0:1, block], (LANES, LANES)))
+            owncol[block, :] = column
+            lane = lax.broadcasted_iota(jnp.int32, (LANES, LANES), 1)
+            for c in range(size // LANES):
+                onehot[block, c * LANES : (c + 1) * LANES] = jnp.where(
+                    column == lane + c * LANES, 1.0, 0.0
+                ).astype(BF16)
+
+    def ordered(at):
+        order(at)
+        return dot(onehot[at, :], coef[...], NT)
+
+    load_seed.wait()
     load_owner.wait()
-
-    def spread(b, carry):
-        at = pl.ds(pl.multiple_of(b * LANES, LANES), LANES)
-        column = jnp.transpose(jnp.broadcast_to(owner_ref[0:1, at], (LANES, LANES)))
-        owncol[at, :] = column
-        lane = lax.broadcasted_iota(jnp.int32, (LANES, LANES), 1)
-        for c in range(size // LANES):
-            onehot[at, c * LANES : (c + 1) * LANES] = jnp.where(
-                column == lane + c * LANES, 1.0, 0.0
-            ).astype(BF16)
-        return carry
-
-    lax.fori_loop(0, size // LANES, spread, 0)
-
-    load_seed.wait()
-    pl.semaphore_wait(barrier, na - 1 + has_low.astype(jnp.int32) + has_high.astype(jnp.int32))
     for k in range(2):
         for c in range(2):
             for s in range(2):
                 g = 2 * c + s
                 coef[g * OWN : (g + 1) * OWN, :] = seed_ref[k + 2 * c, s]
-        stacked(k, onehot, chunk)
+        if k == 0:
+            pl.semaphore_wait(
+                barrier, na - 1 + has_low.astype(jnp.int32) + has_high.astype(jnp.int32)
+            )
+            in_turn(k, chunk, ordered)
+        else:
+            stacked(k, onehot, chunk)
 
     mine = owncol[pl.ds(pl.multiple_of(me * OWN, OWN), OWN), :]
     for c in range(size // LANES):
@@ -324,6 +348,11 @@
     regroup(0, keep_toroidal)
     stacked(2, lat, chunk)
 
+    near, some = na // 4, na // 8
+    recv[4, me] = send[4, pl.ds(pl.multiple_of(me * OWN, OWN), OWN), :]
+    ahead(4, near, some)
+    ahead(4, na - near - some + 1, some)
+
     arrived(1)
 
     def keep_poloidal(g, columns, tile):
@@ -338,7 +367,9 @@
         slope = 0.5 * (fwd_halo[1, at, :].astype(F32) - fwd_halo[0, at, :].astype(F32))
         coef[at, :] = jnp.where(mask[...] > 0.0, slope, 0.0).astype(BF16)
     stacked(3, lat, chunk)
-    scatter(4, 0, na)
+    ahead(4, 1, near - 1)
+    ahead(4, near + some, na - 2 * (near + some) + 1)
+    ahead(4, na - near + 1, near - 1)
 
     def into_grid(base):
         def put(g, columns, tile):

time: 116 us -> 117 us (level); the launches traced: 114 us -> 117 us
  Pallas kernels: 113 us -> 115 us
    pallas_call x1, Pallas kernels: 112 us -> 114 us  [local(): pl.pallas_call(functools.partial(kernel, na, nr), out_shape=(pltpu.VMEM(s...]
where the time goes in v4:
time: 117 us
  Pallas kernels  115 us (98%)
  between operations  1.28 us (1%)
    pallas_call x1, Pallas kernels, local(): pl.pallas_call(functools.partial(kernel, na, nr), out_shape=(pltpu.VMEM(s...  114 us

profile of v4, /device:TPU:1, one launch (start us, length us, event | category | flops | bytes accessed | tf_op | source)
XLA Modules:
  0.0 116.7 jit_solution(8499539841863268326)
XLA Ops:
  1.3 114.3 %shard_map.77 = (f32[2,2,32,1024]{3,2,1,0:T(8,128)S(1)}, f32[4,2,32,1024]{3,2,1,0:T(8,128)S(1)}) custom-call(bf16[4,2,32,1024]{3,2,1,0:T(8,128)(2,1)} %bitcast.9, bf16[2,2,32,1024]{3,2,1,0:T(8,128)(2,1)} %bitcast.10, f32[1]{0:T(128)S(6)} %copy.10.step_hbm, s32[1,1024]{1,0:T(1,128)} %bitcast.11, bf16[1024,1024]{1,0:T(8,128)(2,1)} %constant.4.clone.lat_hbm, ...), custom_call_target="tpu_custom_call" | custom-call | tf_op jit(solution)/shard_map/pallas_call | solution.py:509
  115.5 1.2 %shard_map.78 = (f32[2,2,32,1024]{3,2,1,0:T(8,128)}, f32[4,2,32,1024]{3,2,1,0:T(8,128)}) custom-call(f32[2,2,32,1024]{3,2,1,0:T(8,128)S(1)} %get-tuple-element.6.non_in, f32[4,2,32,1024]{3,2,1,0:T(8,128)S(1)} %get-tuple-element.7.next_in), custom_call_target="tpu_custom_call" | custom-call | tf_op jit(solution)/shard_map/pallas_call | solution.py:552

commit v5 on v4

--- a/solution.py
+++ b/solution.py
@@ -102,12 +102,12 @@
     load_owner.start()
     load_seed.start()
 
-    def greet(step, carry):
-        peer = lax.rem(me + step, na)
+    def greet(i, carry):
+        peer = lax.rem(me + na // 2 + (i + 1) // 2 * (1 - 2 * lax.rem(i, 2)), na)
         pl.semaphore_signal(barrier, inc=1, device_id={"ma": peer}, device_id_type=MESH)
         return carry
 
-    lax.fori_loop(1, na, greet, 0)
+    lax.fori_loop(0, na - 1, greet, 0)
 
     @pl.when(has_low)
     def _():
@@ -164,7 +164,7 @@
         peers = height // OWN
 
         def one(i, carry):
-            turn = lax.rem(me // peers + i, count)
+            turn = lax.rem(me // peers + count // 2 + i + i * (i - 1) // 2, count)
             at = pl.ds(pl.multiple_of(turn * height, height), height)
             send[k, at, :] = rows_of(at).astype(BF16)
             if go:
@@ -435,7 +435,7 @@
     ).astype(BF16)
     analyse(7, tor_grad)
 
-    step = jnp.broadcast_to(step_ref[...].reshape(1, 1), (OWN, chunk))
+    step = jnp.broadcast_to(step_ref[...].reshape(1, 1), (OWN, size))
 
     def finish(k, put):
         arrived(k)
@@ -447,30 +447,18 @@
             halo_sent(rows, fwd_halo, 0)
         regroup(k, keep)
 
-        def one(i, carry):
-            columns = pl.ds(pl.multiple_of(i * chunk, chunk), chunk)
-            result = dot(rows[...], lat[:, columns], NN)
-            live = mask[:, columns] > 0.0
-            for g in range(4):
-                put(
-                    g // 2,
-                    g % 2,
-                    columns,
-                    jnp.where(live, result[g * OWN : (g + 1) * OWN], 0.0),
-                )
-            return carry
-
-        lax.fori_loop(0, size // chunk, one, 0)
-
-    def put_term(s, c, columns, value):
-        non_ref[c, s, :, columns] = value
+        result = dot(rows[...], lat[...], NN)
+        live = mask[...] > 0.0
+        for g in range(4):
+            put(g // 2, g % 2, jnp.where(live, result[g * OWN : (g + 1) * OWN], 0.0))
+
+    def put_term(s, c, value):
+        non_ref[c, s] = value
 
     def put_seed(first):
-        def put(s, c, columns, value):
+        def put(s, c, value):
             channel = 2 * c + first
-            next_ref[channel, s, :, columns] = (
-                listed[channel, s, :, columns].astype(F32) - step * value
-            )
+            next_ref[channel, s] = listed[channel, s].astype(F32) - step * value
 
         return put
 
@@ -483,13 +471,13 @@
 
 
 def settle(non_in, next_in, non_out, next_out, store_sem):
-    stores = [pltpu.make_async_copy(non_in, non_out, store_sem.at[0])]
-    for channel in range(4):
-        stores.append(
-            pltpu.make_async_copy(
-                next_in.at[channel], next_out.at[channel], store_sem.at[channel + 1]
-            )
-        )
+    stores = []
+    for src, dst in ((next_in, next_out), (non_in, non_out)):
+        for c in range(src.shape[0]):
+            for s in range(2):
+                stores.append(
+                    pltpu.make_async_copy(src.at[c, s], dst.at[c, s], store_sem.at[len(stores)])
+                )
     for store in stores:
         store.start()
     for store in stores:
@@ -555,7 +543,7 @@
         in_specs=[hbm] * 2,
         out_specs=(hbm, hbm),
         scratch_shapes=[
-            pltpu.SemaphoreType.DMA((5,)),
+            pltpu.SemaphoreType.DMA((12,)),
         ],
         compiler_params=pltpu.CompilerParams(vmem_limit_bytes=40 << 20),
     )(*outputs)

time: 117 us -> 112 us (0.957)
  Pallas kernels: 115 us -> 111 us
    pallas_call x1, Pallas kernels: 114 us -> 109 us  [local(): pl.pallas_call(functools.partial(kernel, na, nr), out_shape=(pltpu.VMEM(s...]
where the time goes in v5:
time: 112 us
  Pallas kernels  111 us (99%)
  between operations  1.28 us (1%)
    pallas_call x1, Pallas kernels, local(): pl.pallas_call(functools.partial(kernel, na, nr), out_shape=(pltpu.VMEM(s...  109 us

profile of v5, /device:TPU:1, one launch (start us, length us, event | category | flops | bytes accessed | tf_op | source)
XLA Modules:
  0.0 111.8 jit_solution(4971802306519231191)
XLA Ops:
  1.3 109.3 %shard_map.77 = (f32[2,2,32,1024]{3,2,1,0:T(8,128)S(1)}, f32[4,2,32,1024]{3,2,1,0:T(8,128)S(1)}) custom-call(bf16[4,2,32,1024]{3,2,1,0:T(8,128)(2,1)} %bitcast.9, bf16[2,2,32,1024]{3,2,1,0:T(8,128)(2,1)} %bitcast.10, f32[1]{0:T(128)S(6)} %copy.10.step_hbm, s32[1,1024]{1,0:T(1,128)} %bitcast.11, bf16[1024,1024]{1,0:T(8,128)(2,1)} %constant.4.clone.lat_hbm, ...), custom_call_target="tpu_custom_call" | custom-call | tf_op jit(solution)/shard_map/pallas_call | solution.py:497
  110.6 1.2 %shard_map.78 = (f32[2,2,32,1024]{3,2,1,0:T(8,128)}, f32[4,2,32,1024]{3,2,1,0:T(8,128)}) custom-call(f32[2,2,32,1024]{3,2,1,0:T(8,128)S(1)} %get-tuple-element.6.non_in, f32[4,2,32,1024]{3,2,1,0:T(8,128)S(1)} %get-tuple-element.7.next_in), custom_call_target="tpu_custom_call" | custom-call | tf_op jit(solution)/shard_map/pallas_call | solution.py:540

commit v6 on v5

--- a/solution.py
+++ b/solution.py
@@ -102,9 +102,11 @@
     load_owner.start()
     load_seed.start()
 
+    def farthest(i):
+        return lax.rem(me + na // 2 + (i + 1) // 2 * (1 - 2 * lax.rem(i, 2)), na)
+
     def greet(i, carry):
-        peer = lax.rem(me + na // 2 + (i + 1) // 2 * (1 - 2 * lax.rem(i, 2)), na)
-        pl.semaphore_signal(barrier, inc=1, device_id={"ma": peer}, device_id_type=MESH)
+        pl.semaphore_signal(barrier, inc=1, device_id={"ma": farthest(i)}, device_id_type=MESH)
         return carry
 
     lax.fori_loop(0, na - 1, greet, 0)
@@ -120,46 +122,36 @@
     for load in loads[2:]:
         load.start()
 
-    def scatter(k, first, count):
+    def send_block(k, peer):
+        pltpu.make_async_remote_copy(
+            src_ref=send.at[k, pl.ds(pl.multiple_of(peer * OWN, OWN), OWN), :],
+            dst_ref=recv.at[k, me],
+            send_sem=send_sem.at[k],
+            recv_sem=recv_sem.at[k],
+            device_id={"ma": peer},
+            device_id_type=MESH,
+        ).start()
+
+    def keep_own(k):
+        recv[k, me] = send[k, pl.ds(pl.multiple_of(me * OWN, OWN), OWN), :]
+
+    def scatter(k, first, last):
         def one(i, carry):
-            peer = first + i
-            block = send.at[k, pl.ds(pl.multiple_of(peer * OWN, OWN), OWN), :]
-
-            @pl.when(peer != me)
-            def _():
-                pltpu.make_async_remote_copy(
-                    src_ref=block,
-                    dst_ref=recv.at[k, me],
-                    send_sem=send_sem.at[k],
-                    recv_sem=recv_sem.at[k],
-                    device_id={"ma": peer},
-                    device_id_type=MESH,
-                ).start()
-
-            @pl.when(peer == me)
-            def _():
-                recv[k, me] = block[...]
-
+            send_block(k, farthest(i))
             return carry
 
-        lax.fori_loop(0, count, one, 0)
-
-    def ahead(k, first, count):
+        lax.fori_loop(first, last, one, 0)
+
+    def made(k, height, rows_of):
         def one(i, carry):
-            peer = lax.rem(me + first + i, na)
-            pltpu.make_async_remote_copy(
-                src_ref=send.at[k, pl.ds(pl.multiple_of(peer * OWN, OWN), OWN), :],
-                dst_ref=recv.at[k, me],
-                send_sem=send_sem.at[k],
-                recv_sem=recv_sem.at[k],
-                device_id={"ma": peer},
-                device_id_type=MESH,
-            ).start()
+            at = pl.ds(pl.multiple_of(i * height, height), height)
+            send[k, at, :] = rows_of(at).astype(BF16)
             return carry
 
-        lax.fori_loop(0, count, one, 0)
-
-    def in_turn(k, height, rows_of, go=True):
+        lax.fori_loop(0, size // height, one, 0)
+        keep_own(k)
+
+    def made_in_turn(k, height, rows_of):
         count = size // height
         peers = height // OWN
 
@@ -167,11 +159,21 @@
             turn = lax.rem(me // peers + count // 2 + i + i * (i - 1) // 2, count)
             at = pl.ds(pl.multiple_of(turn * height, height), height)
             send[k, at, :] = rows_of(at).astype(BF16)
-            if go:
-                scatter(k, turn * peers, peers)
+
+            def block(j, carry):
+                peer = turn * peers + j
+
+                @pl.when(peer != me)
+                def _():
+                    send_block(k, peer)
+
+                return carry
+
+            lax.fori_loop(0, peers, block, 0)
             return carry
 
         lax.fori_loop(0, count, one, 0)
+        keep_own(k)
 
     def arrived(k):
         part = recv.at[k, pl.ds(0, na - 1)]
@@ -271,8 +273,8 @@
 
         lax.fori_loop(0, quads, one, 0, unroll=min(4, quads))
 
-    def stacked(k, left, height, go=True):
-        in_turn(k, height, lambda at: dot(left[at, :], coef[...], NT), go)
+    def stacked(k, left):
+        made(k, tall, lambda at: dot(left[at, :], coef[...], NT))
 
     def order(at):
         for b in range(at.size // LANES):
@@ -300,9 +302,10 @@
             pl.semaphore_wait(
                 barrier, na - 1 + has_low.astype(jnp.int32) + has_high.astype(jnp.int32)
             )
-            in_turn(k, chunk, ordered)
+            made_in_turn(k, chunk, ordered)
         else:
-            stacked(k, onehot, chunk)
+            stacked(k, onehot)
+            scatter(k, 0, na - 1)
 
     mine = owncol[pl.ds(pl.multiple_of(me * OWN, OWN), OWN), :]
     for c in range(size // LANES):
@@ -318,7 +321,7 @@
             coef[g * OWN : (g + 1) * OWN, :] = jnp.where(
                 mask[...] > 0.0, cot_ref[c, s].astype(F32), 0.0
             ).astype(BF16)
-    stacked(4, lat, tall, go=False)
+    stacked(4, lat)
 
     load_wave.wait()
     part = min(512, points)
@@ -346,12 +349,11 @@
         ).astype(BF16)
 
     regroup(0, keep_toroidal)
-    stacked(2, lat, chunk)
-
-    near, some = na // 4, na // 8
-    recv[4, me] = send[4, pl.ds(pl.multiple_of(me * OWN, OWN), OWN), :]
-    ahead(4, near, some)
-    ahead(4, na - near - some + 1, some)
+    stacked(2, lat)
+    scatter(2, 0, na - 1)
+
+    early, late = na // 4 + 1, na // 2 + 1
+    scatter(4, early, late)
 
     arrived(1)
 
@@ -366,10 +368,10 @@
         at = slice(g * OWN, (g + 1) * OWN)
         slope = 0.5 * (fwd_halo[1, at, :].astype(F32) - fwd_halo[0, at, :].astype(F32))
         coef[at, :] = jnp.where(mask[...] > 0.0, slope, 0.0).astype(BF16)
-    stacked(3, lat, chunk)
-    ahead(4, 1, near - 1)
-    ahead(4, near + some, na - 2 * (near + some) + 1)
-    ahead(4, na - near + 1, near - 1)
+    stacked(3, lat)
+    scatter(3, 0, na - 1)
+    scatter(4, 0, early)
+    scatter(4, late, na - 1)
 
     def into_grid(base):
         def put(g, columns, tile):
@@ -403,11 +405,12 @@
         return carry
 
     def analyse(k, source):
-        def made(at):
+        def analysed(at):
             parts = [dot(table[s, at, :], source[...], NT) for s in range(2)]
             return scale * jnp.concatenate(parts, axis=1)
 
-        in_turn(k, tall, made)
+        made(k, tall, analysed)
+        scatter(k, 0, na - 1)
 
     lax.fori_loop(0, points // wide, terms, 0)
     analyse(5, back_send)

time: 112 us -> 112 us (level)
  no operation moved by 1% of the time
where the time goes in v6:
time: 112 us
  Pallas kernels  111 us (99%)
  between operations  1.28 us (1%)
    pallas_call x1, Pallas kernels, local(): pl.pallas_call(functools.partial(kernel, na, nr), out_shape=(pltpu.VMEM(s...  110 us

profile of v6, /device:TPU:1, one launch (start us, length us, event | category | flops | bytes accessed | tf_op | source)
XLA Modules:
  0.0 112.1 jit_solution(1387094689947557083)
XLA Ops:
  1.3 109.6 %shard_map.77 = (f32[2,2,32,1024]{3,2,1,0:T(8,128)S(1)}, f32[4,2,32,1024]{3,2,1,0:T(8,128)S(1)}) custom-call(bf16[4,2,32,1024]{3,2,1,0:T(8,128)(2,1)} %bitcast.9, bf16[2,2,32,1024]{3,2,1,0:T(8,128)(2,1)} %bitcast.10, f32[1]{0:T(128)S(6)} %copy.10.step_hbm, s32[1,1024]{1,0:T(1,128)} %bitcast.11, bf16[1024,1024]{1,0:T(8,128)(2,1)} %constant.4.clone.lat_hbm, ...), custom_call_target="tpu_custom_call" | custom-call | tf_op jit(solution)/shard_map/pallas_call | solution.py:500
  110.9 1.2 %shard_map.78 = (f32[2,2,32,1024]{3,2,1,0:T(8,128)}, f32[4,2,32,1024]{3,2,1,0:T(8,128)}) custom-call(f32[2,2,32,1024]{3,2,1,0:T(8,128)S(1)} %get-tuple-element.6.non_in, f32[4,2,32,1024]{3,2,1,0:T(8,128)S(1)} %get-tuple-element.7.next_in), custom_call_target="tpu_custom_call" | custom-call | tf_op jit(solution)/shard_map/pallas_call | solution.py:543

commit v7 on v6

--- a/solution.py
+++ b/solution.py
@@ -299,13 +299,13 @@
                 g = 2 * c + s
                 coef[g * OWN : (g + 1) * OWN, :] = seed_ref[k + 2 * c, s]
         if k == 0:
+            made(k, chunk, ordered)
             pl.semaphore_wait(
                 barrier, na - 1 + has_low.astype(jnp.int32) + has_high.astype(jnp.int32)
             )
-            made_in_turn(k, chunk, ordered)
         else:
             stacked(k, onehot)
-            scatter(k, 0, na - 1)
+        scatter(k, 0, na - 1)
 
     mine = owncol[pl.ds(pl.multiple_of(me * OWN, OWN), OWN), :]
     for c in range(size // LANES):
@@ -349,8 +349,7 @@
         ).astype(BF16)
 
     regroup(0, keep_toroidal)
-    stacked(2, lat)
-    scatter(2, 0, na - 1)
+    made_in_turn(2, chunk, lambda at: dot(lat[at, :], coef[...], NT))
 
     early, late = na // 4 + 1, na // 2 + 1
     scatter(4, early, late)
@@ -368,8 +367,7 @@
         at = slice(g * OWN, (g + 1) * OWN)
         slope = 0.5 * (fwd_halo[1, at, :].astype(F32) - fwd_halo[0, at, :].astype(F32))
         coef[at, :] = jnp.where(mask[...] > 0.0, slope, 0.0).astype(BF16)
-    stacked(3, lat)
-    scatter(3, 0, na - 1)
+    made_in_turn(3, chunk, lambda at: dot(lat[at, :], coef[...], NT))
     scatter(4, 0, early)
     scatter(4, late, na - 1)
 
@@ -409,8 +407,7 @@
             parts = [dot(table[s, at, :], source[...], NT) for s in range(2)]
             return scale * jnp.concatenate(parts, axis=1)
 
-        made(k, tall, analysed)
-        scatter(k, 0, na - 1)
+        made_in_turn(k, tall, analysed)
 
     lax.fori_loop(0, points // wide, terms, 0)
     analyse(5, back_send)

time: 112 us -> 111 us (level)
  no operation moved by 1% of the time
where the time goes in v7:
time: 111 us
  Pallas kernels  110 us (99%)
  between operations  1.28 us (1%)
    pallas_call x1, Pallas kernels, local(): pl.pallas_call(functools.partial(kernel, na, nr), out_shape=(pltpu.VMEM(s...  109 us

profile of v7, /device:TPU:1, one launch (start us, length us, event | category | flops | bytes accessed | tf_op | source)
XLA Modules:
  0.0 111.1 jit_solution(4214466135336104913)
XLA Ops:
  1.3 108.6 %shard_map.77 = (f32[2,2,32,1024]{3,2,1,0:T(8,128)S(1)}, f32[4,2,32,1024]{3,2,1,0:T(8,128)S(1)}) custom-call(bf16[4,2,32,1024]{3,2,1,0:T(8,128)(2,1)} %bitcast.9, bf16[2,2,32,1024]{3,2,1,0:T(8,128)(2,1)} %bitcast.10, f32[1]{0:T(128)S(6)} %copy.10.step_hbm, s32[1,1024]{1,0:T(1,128)} %bitcast.11, bf16[1024,1024]{1,0:T(8,128)(2,1)} %constant.4.clone.lat_hbm, ...), custom_call_target="tpu_custom_call" | custom-call | tf_op jit(solution)/shard_map/pallas_call | solution.py:497
  109.9 1.2 %shard_map.78 = (f32[2,2,32,1024]{3,2,1,0:T(8,128)}, f32[4,2,32,1024]{3,2,1,0:T(8,128)}) custom-call(f32[2,2,32,1024]{3,2,1,0:T(8,128)S(1)} %get-tuple-element.6.non_in, f32[4,2,32,1024]{3,2,1,0:T(8,128)S(1)} %get-tuple-element.7.next_in), custom_call_target="tpu_custom_call" | custom-call | tf_op jit(solution)/shard_map/pallas_call | solution.py:540

commit v8 on v7

--- a/solution.py
+++ b/solution.py
@@ -58,6 +58,7 @@
     coef,
     listed,
     rows,
+    spec,
     grid,
     field,
     fwd_halo,
@@ -358,16 +359,25 @@
 
     def keep_poloidal(g, columns, tile):
         listed[2 * (g // 2) + 1, g % 2, :, columns] = tile.astype(BF16)
-        rows[g * OWN : (g + 1) * OWN, columns] = tile.astype(BF16)
+        coef[g * OWN : (g + 1) * OWN, columns] = jnp.where(
+            mask[:, columns] > 0.0, tile, 0.0
+        ).astype(BF16)
 
     regroup(1, keep_poloidal)
-    halo_start(rows, fwd_halo, 0)
-    halo_wait(rows, fwd_halo, 0)
-    for g in range(4):
-        at = slice(g * OWN, (g + 1) * OWN)
-        slope = 0.5 * (fwd_halo[1, at, :].astype(F32) - fwd_halo[0, at, :].astype(F32))
-        coef[at, :] = jnp.where(mask[...] > 0.0, slope, 0.0).astype(BF16)
-    made_in_turn(3, chunk, lambda at: dot(lat[at, :], coef[...], NT))
+
+    def poloidal(i, carry):
+        at = pl.ds(pl.multiple_of(i * tall, tall), tall)
+        spec[at, :] = dot(lat[at, :], coef[...], NT).astype(BF16)
+        return carry
+
+    lax.fori_loop(0, size // tall, poloidal, 0)
+    halo_start(spec, fwd_halo, 0)
+    halo_wait(spec, fwd_halo, 0)
+    made_in_turn(
+        3,
+        chunk,
+        lambda at: 0.5 * (fwd_halo[1, at, :].astype(F32) - fwd_halo[0, at, :].astype(F32)),
+    )
     scatter(4, 0, early)
     scatter(4, late, na - 1)
 
@@ -444,7 +454,7 @@
             rows[g * OWN : (g + 1) * OWN, columns] = tile.astype(BF16)
 
         if k == 5:
-            halo_sent(rows, fwd_halo, 0)
+            halo_sent(spec, fwd_halo, 0)
         regroup(k, keep)
 
         result = dot(rows[...], lat[...], NN)
@@ -513,9 +523,10 @@
             pltpu.VMEM((4 * OWN, size), BF16),
             pltpu.VMEM((4, 2, OWN, size), BF16),
             pltpu.VMEM((4 * OWN, size), BF16),
+            pltpu.VMEM((size, LANES), BF16),
             pltpu.VMEM((6, 2, OWN, size), BF16),
             pltpu.VMEM((4, OWN, points), F32),
-            pltpu.VMEM((2, 4 * OWN, size), BF16),
+            pltpu.VMEM((2, size, LANES), BF16),
             pltpu.VMEM((2 * OWN, points), BF16),
             pltpu.VMEM((3, 2 * OWN, points), BF16),
             pltpu.VMEM((8, size, LANES), BF16),

time: 111 us -> 111 us (level)
  no operation moved by 1% of the time
where the time goes in v8:
time: 111 us
  Pallas kernels  110 us (99%)
  between operations  1.28 us (1%)
    pallas_call x1, Pallas kernels, local(): pl.pallas_call(functools.partial(kernel, na, nr), out_shape=(pltpu.VMEM(s...  109 us

profile of v8, /device:TPU:1, one launch (start us, length us, event | category | flops | bytes accessed | tf_op | source)
XLA Modules:
  0.0 111.2 jit_solution(4759222492366301564)
XLA Ops:
  1.3 108.6 %shard_map.77 = (f32[2,2,32,1024]{3,2,1,0:T(8,128)S(1)}, f32[4,2,32,1024]{3,2,1,0:T(8,128)S(1)}) custom-call(bf16[4,2,32,1024]{3,2,1,0:T(8,128)(2,1)} %bitcast.9, bf16[2,2,32,1024]{3,2,1,0:T(8,128)(2,1)} %bitcast.10, f32[1]{0:T(128)S(6)} %copy.10.step_hbm, s32[1,1024]{1,0:T(1,128)} %bitcast.11, bf16[1024,1024]{1,0:T(8,128)(2,1)} %constant.4.clone.lat_hbm, ...), custom_call_target="tpu_custom_call" | custom-call | tf_op jit(solution)/shard_map/pallas_call | solution.py:507
  109.9 1.2 %shard_map.78 = (f32[2,2,32,1024]{3,2,1,0:T(8,128)}, f32[4,2,32,1024]{3,2,1,0:T(8,128)}) custom-call(f32[2,2,32,1024]{3,2,1,0:T(8,128)S(1)} %get-tuple-element.6.non_in, f32[4,2,32,1024]{3,2,1,0:T(8,128)S(1)} %get-tuple-element.7.next_in), custom_call_target="tpu_custom_call" | custom-call | tf_op jit(solution)/shard_map/pallas_call | solution.py:551
